TPU v7x, 32 devices: a whole 2x2x4 slice. The times are simulated.
32 devices in a mesh: seq: 4 (over x, core), shard: 8 (over z, y).
Axes of the slice: x: 2, y: 2, z: 4, core: 2. Of those that a mesh axis runs over, the one named last changes fastest.
Arguments:
- inputs: bfloat16 [16, 584, 1024], P('shard', 'seq'), may hold values from -6 to 6
- key_mask: int32 [16, 584], P('shard'), may hold values from 0 to 1, as said below
- cotangent: bfloat16 [16, 584, 1024], P('shard', 'seq'), may hold values from -6 to 6
- attn_gain: bfloat16 [1024], P('shard'), may hold values from 0.5 to 1.5
- attn_shift: bfloat16 [1024], P('shard'), may hold values from -1.796875 to 1.796875
- qkv_weight: bfloat16 [1024, 3072], P('shard'), may hold values from -0.1875 to 0.1875
- query_bias: bfloat16 [1024], P('shard'), may hold values from -1.796875 to 1.796875
- value_bias: bfloat16 [1024], P('shard'), may hold values from -1.796875 to 1.796875
- out_weight: bfloat16 [1024, 1024], P('shard'), may hold values from -2 to 2
- out_bias: bfloat16 [1024], P('shard'), may hold values from -1.796875 to 1.796875
- mlp_gain: bfloat16 [1024], P('shard'), may hold values from 0.5 to 1.5
- mlp_shift: bfloat16 [1024], P('shard'), may hold values from -1.796875 to 1.796875
- up_weight: bfloat16 [1024, 4096], P('shard'), may hold values from -0.1875 to 0.1875
- up_bias: bfloat16 [4096], P('shard'), may hold values from -1.796875 to 1.796875
- down_weight: bfloat16 [4096, 1024], P('shard'), may hold values from -0.125 to 0.125
- down_bias: bfloat16 [1024], P('shard'), may hold values from -1.796875 to 1.796875
Outputs:
- output: bfloat16 [16, 584, 1024], P('shard', 'seq')
- input_grad: bfloat16 [16, 584, 1024], P('shard', 'seq')
- grad_attn_gain: float32 [1024], P('shard')
- grad_attn_shift: float32 [1024], P('shard')
- grad_qkv_weight: float32 [1024, 3072], P('shard')
- grad_query_bias: float32 [1024], P('shard')
- grad_value_bias: float32 [1024], P('shard')
- grad_out_weight: float32 [1024, 1024], P('shard')
- grad_out_bias: float32 [1024], P('shard')
- grad_mlp_gain: float32 [1024], P('shard')
- grad_mlp_shift: float32 [1024], P('shard')
- grad_up_weight: float32 [1024, 4096], P('shard')
- grad_up_bias: float32 [4096], P('shard')
- grad_down_weight: float32 [4096, 1024], P('shard')
- grad_down_bias: float32 [1024], P('shard')
Inputs may be any that keep to these rules, and one draw needn't show every extreme that they name: `key_mask`: each image has exactly 577 ones, at positions that differ from image to image.
All inputs are finite; a program needn't handle non-finite values.
Results may differ from a plain program's by a relative error of at most 0.02.
Values may be sent and summed in bfloat16 or wider, within the bound.
A program may use at most 192 MiB of HBM per device.

v0:
```python
import jax
import jax.numpy as jnp
from jax import lax
from jax.sharding import PartitionSpec as P

D = 1024
HEAD_DIM = 64


EPSILON = 1e-05


def product(left, right):
    return jnp.dot(left, right, preferred_element_type=jnp.float32)


def product_tn(left, right):
    return lax.dot_general(
        left, right, (((0,), (0,)), ((), ())), preferred_element_type=jnp.float32
    )


def product_nt(left, right):
    return lax.dot_general(
        left, right, (((1,), (1,)), ((), ())), preferred_element_type=jnp.float32
    )


def norm_rows(current, gain, shift):
    centre = jnp.mean(current, axis=-1, keepdims=True)
    centred = current - centre
    inverse = lax.rsqrt(jnp.mean(centred * centred, axis=-1, keepdims=True) + EPSILON)
    scaled = centred * inverse
    return (scaled * gain + shift, scaled, inverse)


def norm_back(incoming, scaled, inverse, gain):
    inner = incoming * gain
    d_current = inverse * (
        inner
        - jnp.mean(inner, axis=-1, keepdims=True)
        - scaled * jnp.mean(inner * scaled, axis=-1, keepdims=True)
    )
    return (d_current, jnp.sum(incoming * scaled, axis=0), jnp.sum(incoming, axis=0))


def split_heads(block):
    images, length, width = block.shape
    return block.reshape(images, length, width // HEAD_DIM, HEAD_DIM)


def masked_scores(query_h, keyed_h, key_mask):
    scores = jnp.einsum("iqhd,ikhd->ihqk", query_h, keyed_h, preferred_element_type=jnp.float32)
    scores = scores * HEAD_DIM ** (-0.5)
    return jnp.where(key_mask[:, None, None, :] > 0, scores, -1e30)


def layer_forward(current, key_mask, weights, images):
    (
        attn_gain,
        attn_shift,
        qkv_weight,
        query_bias,
        value_bias,
        out_weight,
        out_bias,
        mlp_gain,
        mlp_shift,
        up_weight,
        up_bias,
        down_weight,
        down_bias,
    ) = weights
    row_count = current.shape[0]
    tok_local = row_count // images
    normed, scaled_a, inverse_a = norm_rows(
        current, attn_gain.astype(jnp.float32), attn_shift.astype(jnp.float32)
    )
    normed_low = normed.astype(jnp.bfloat16)
    packed_bias = jnp.concatenate(
        [
            query_bias.astype(jnp.float32),
            jnp.zeros((D,), jnp.float32),
            value_bias.astype(jnp.float32),
        ]
    )
    packed = (product(normed_low, qkv_weight) + packed_bias).astype(jnp.bfloat16)
    packed = packed.reshape(images, tok_local, 3, D)
    head_view = lax.all_to_all(packed, "seq", split_axis=3, concat_axis=1, tiled=True)
    query_h = split_heads(head_view[:, :, 0])
    keyed_h = split_heads(head_view[:, :, 1])
    value_h = split_heads(head_view[:, :, 2])
    scores = masked_scores(query_h, keyed_h, key_mask)
    row_max = jnp.max(scores, axis=-1, keepdims=True)
    raised = jnp.exp(scores - row_max)
    row_sum = jnp.sum(raised, axis=-1, keepdims=True)
    attn_probs = raised / row_sum
    log_total = row_max + jnp.log(row_sum)
    mixed = jnp.einsum(
        "ihqk,ikhd->iqhd",
        attn_probs.astype(jnp.bfloat16),
        value_h,
        preferred_element_type=jnp.float32,
    )
    seq_len = head_view.shape[1]
    mixed = mixed.reshape(images, seq_len, head_view.shape[3]).astype(jnp.bfloat16)
    merged = lax.all_to_all(mixed, "seq", split_axis=1, concat_axis=2, tiled=True)
    merged_rows = merged.reshape(row_count, D)
    middle = current + product(merged_rows, out_weight) + out_bias.astype(jnp.float32)
    second, scaled_b, inverse_b = norm_rows(
        middle, mlp_gain.astype(jnp.float32), mlp_shift.astype(jnp.float32)
    )
    second_low = second.astype(jnp.bfloat16)
    hidden = product(second_low, up_weight) + up_bias.astype(jnp.float32)
    active = (hidden * jax.nn.sigmoid(1.702 * hidden)).astype(jnp.bfloat16)
    result = middle + product(active, down_weight) + down_bias.astype(jnp.float32)
    stored = (
        scaled_a,
        inverse_a,
        normed_low,
        head_view,
        log_total,
        merged_rows,
        scaled_b,
        inverse_b,
        second_low,
        hidden,
        active,
    )
    return (result, stored)


def layer_backward(upstream, key_mask, weights, stored, images):
    (
        attn_gain,
        attn_shift,
        qkv_weight,
        query_bias,
        value_bias,
        out_weight,
        out_bias,
        mlp_gain,
        mlp_shift,
        up_weight,
        up_bias,
        down_weight,
        down_bias,
    ) = weights
    (
        scaled_a,
        inverse_a,
        normed_low,
        head_view,
        log_total,
        merged_rows,
        scaled_b,
        inverse_b,
        second_low,
        hidden,
        active,
    ) = stored
    row_count = upstream.shape[0]
    tok_local = row_count // images
    branch_low = upstream.astype(jnp.bfloat16)
    grad_down_bias = jnp.sum(branch_low, axis=0, dtype=jnp.float32)
    grad_down_weight = product_tn(active, branch_low)
    d_active = product_nt(branch_low, down_weight)
    gate_sig = jax.nn.sigmoid(1.702 * hidden)
    d_hidden = (d_active * (gate_sig + 1.702 * hidden * gate_sig * (1.0 - gate_sig))).astype(
        jnp.bfloat16
    )
    grad_up_bias = jnp.sum(d_hidden, axis=0, dtype=jnp.float32)
    grad_up_weight = product_tn(second_low, d_hidden)
    d_second = product_nt(d_hidden, up_weight)
    d_norm_b, grad_mlp_gain, grad_mlp_shift = norm_back(
        d_second, scaled_b, inverse_b, mlp_gain.astype(jnp.float32)
    )
    d_middle = upstream + d_norm_b
    d_branch = d_middle.astype(jnp.bfloat16)
    grad_out_bias = jnp.sum(d_branch, axis=0, dtype=jnp.float32)
    grad_out_weight = product_tn(merged_rows, d_branch)
    d_merged = product_nt(d_branch, out_weight).astype(jnp.bfloat16).reshape(images, tok_local, D)
    d_heads = lax.all_to_all(d_merged, "seq", split_axis=2, concat_axis=1, tiled=True)
    query_h = split_heads(head_view[:, :, 0])
    keyed_h = split_heads(head_view[:, :, 1])
    value_h = split_heads(head_view[:, :, 2])
    d_out_h = split_heads(d_heads)
    scores = masked_scores(query_h, keyed_h, key_mask)
    attn_probs = jnp.exp(scores - log_total)
    d_value = jnp.einsum(
        "ihqk,iqhd->ikhd",
        attn_probs.astype(jnp.bfloat16),
        d_out_h,
        preferred_element_type=jnp.float32,
    )
    d_probs = jnp.einsum("iqhd,ikhd->ihqk", d_out_h, value_h, preferred_element_type=jnp.float32)
    d_scores = attn_probs * (d_probs - jnp.sum(attn_probs * d_probs, axis=-1, keepdims=True))
    d_scores = d_scores.astype(jnp.bfloat16)
    d_query = jnp.einsum(
        "ihqk,ikhd->iqhd", d_scores, keyed_h, preferred_element_type=jnp.float32
    ) * HEAD_DIM ** (-0.5)
    d_key = jnp.einsum(
        "ihqk,iqhd->ikhd", d_scores, query_h, preferred_element_type=jnp.float32
    ) * HEAD_DIM ** (-0.5)
    seq_len = head_view.shape[1]
    d_packed = jnp.stack((d_query, d_key, d_value), axis=2).astype(jnp.bfloat16)
    d_packed = d_packed.reshape(images, seq_len, 3, head_view.shape[3])
    d_tokens = lax.all_to_all(d_packed, "seq", split_axis=1, concat_axis=3, tiled=True).reshape(
        row_count, 3 * D
    )
    grad_query_bias = jnp.sum(d_tokens[:, :D], axis=0, dtype=jnp.float32)
    grad_value_bias = jnp.sum(d_tokens[:, 2 * D :], axis=0, dtype=jnp.float32)
    grad_qkv_weight = product_tn(normed_low, d_tokens)
    d_normed = product_nt(d_tokens, qkv_weight)
    d_norm_a, grad_attn_gain, grad_attn_shift = norm_back(
        d_normed, scaled_a, inverse_a, attn_gain.astype(jnp.float32)
    )
    grads = (
        grad_attn_gain,
        grad_attn_shift,
        grad_qkv_weight,
        grad_query_bias,
        grad_value_bias,
        grad_out_weight,
        grad_out_bias,
        grad_mlp_gain,
        grad_mlp_shift,
        grad_up_weight,
        grad_up_bias,
        grad_down_weight,
        grad_down_bias,
    )
    return (d_middle + d_norm_a, grads)


def reduce_grads(grads):
    shares = (
        lax.psum_scatter(
            grads[0].astype(jnp.bfloat16), "shard", scatter_dimension=0, tiled=True
        ).astype(jnp.float32),
        lax.psum_scatter(
            grads[1].astype(jnp.bfloat16), "shard", scatter_dimension=0, tiled=True
        ).astype(jnp.float32),
        lax.psum_scatter(
            grads[2].astype(jnp.bfloat16), "shard", scatter_dimension=0, tiled=True
        ).astype(jnp.float32),
        lax.psum_scatter(
            grads[3].astype(jnp.bfloat16), "shard", scatter_dimension=0, tiled=True
        ).astype(jnp.float32),
        lax.psum_scatter(
            grads[4].astype(jnp.bfloat16), "shard", scatter_dimension=0, tiled=True
        ).astype(jnp.float32),
        lax.psum_scatter(
            grads[5].astype(jnp.bfloat16), "shard", scatter_dimension=0, tiled=True
        ).astype(jnp.float32),
        lax.psum_scatter(
            grads[6].astype(jnp.bfloat16), "shard", scatter_dimension=0, tiled=True
        ).astype(jnp.float32),
        lax.psum_scatter(
            grads[7].astype(jnp.bfloat16), "shard", scatter_dimension=0, tiled=True
        ).astype(jnp.float32),
        lax.psum_scatter(
            grads[8].astype(jnp.bfloat16), "shard", scatter_dimension=0, tiled=True
        ).astype(jnp.float32),
        lax.psum_scatter(
            grads[9].astype(jnp.bfloat16), "shard", scatter_dimension=0, tiled=True
        ).astype(jnp.float32),
        lax.psum_scatter(
            grads[10].astype(jnp.bfloat16), "shard", scatter_dimension=0, tiled=True
        ).astype(jnp.float32),
        lax.psum_scatter(
            grads[11].astype(jnp.bfloat16), "shard", scatter_dimension=0, tiled=True
        ).astype(jnp.float32),
        lax.psum_scatter(
            grads[12].astype(jnp.bfloat16), "shard", scatter_dimension=0, tiled=True
        ).astype(jnp.float32),
    )
    return (
        lax.psum(shares[0].astype(jnp.bfloat16), "seq").astype(jnp.float32),
        lax.psum(shares[1].astype(jnp.bfloat16), "seq").astype(jnp.float32),
        lax.psum(shares[2].astype(jnp.bfloat16), "seq").astype(jnp.float32),
        lax.psum(shares[3].astype(jnp.bfloat16), "seq").astype(jnp.float32),
        lax.psum(shares[4].astype(jnp.bfloat16), "seq").astype(jnp.float32),
        lax.psum(shares[5].astype(jnp.bfloat16), "seq").astype(jnp.float32),
        lax.psum(shares[6].astype(jnp.bfloat16), "seq").astype(jnp.float32),
        lax.psum(shares[7].astype(jnp.bfloat16), "seq").astype(jnp.float32),
        lax.psum(shares[8].astype(jnp.bfloat16), "seq").astype(jnp.float32),
        lax.psum(shares[9].astype(jnp.bfloat16), "seq").astype(jnp.float32),
        lax.psum(shares[10].astype(jnp.bfloat16), "seq").astype(jnp.float32),
        lax.psum(shares[11].astype(jnp.bfloat16), "seq").astype(jnp.float32),
        lax.psum(shares[12].astype(jnp.bfloat16), "seq").astype(jnp.float32),
    )


def per_device(
    inputs,
    key_mask,
    cotangent,
    attn_gain,
    attn_shift,
    qkv_weight,
    query_bias,
    value_bias,
    out_weight,
    out_bias,
    mlp_gain,
    mlp_shift,
    up_weight,
    up_bias,
    down_weight,
    down_bias,
):
    shard_set = (
        attn_gain,
        attn_shift,
        qkv_weight,
        query_bias,
        value_bias,
        out_weight,
        out_bias,
        mlp_gain,
        mlp_shift,
        up_weight,
        up_bias,
        down_weight,
        down_bias,
    )
    images = inputs.shape[0]
    tok_local = inputs.shape[1]
    row_count = images * tok_local
    current = inputs.astype(jnp.float32).reshape(row_count, D)
    gathered = (
        lax.all_gather(shard_set[0], "shard", axis=0, tiled=True),
        lax.all_gather(shard_set[1], "shard", axis=0, tiled=True),
        lax.all_gather(shard_set[2], "shard", axis=0, tiled=True),
        lax.all_gather(shard_set[3], "shard", axis=0, tiled=True),
        lax.all_gather(shard_set[4], "shard", axis=0, tiled=True),
        lax.all_gather(shard_set[5], "shard", axis=0, tiled=True),
        lax.all_gather(shard_set[6], "shard", axis=0, tiled=True),
        lax.all_gather(shard_set[7], "shard", axis=0, tiled=True),
        lax.all_gather(shard_set[8], "shard", axis=0, tiled=True),
        lax.all_gather(shard_set[9], "shard", axis=0, tiled=True),
        lax.all_gather(shard_set[10], "shard", axis=0, tiled=True),
        lax.all_gather(shard_set[11], "shard", axis=0, tiled=True),
        lax.all_gather(shard_set[12], "shard", axis=0, tiled=True),
    )
    result, stored = layer_forward(current, key_mask, gathered, images)
    output = result.astype(jnp.bfloat16).reshape(images, tok_local, D)
    start_row = lax.axis_index("seq") * tok_local
    own_mask = lax.dynamic_slice_in_dim(key_mask, start_row, tok_local, 1).astype(jnp.float32)
    upstream = (cotangent.astype(jnp.float32) * own_mask[:, :, None]).reshape(row_count, D)
    again = (
        lax.all_gather(shard_set[0], "shard", axis=0, tiled=True),
        lax.all_gather(shard_set[1], "shard", axis=0, tiled=True),
        lax.all_gather(shard_set[2], "shard", axis=0, tiled=True),
        lax.all_gather(shard_set[3], "shard", axis=0, tiled=True),
        lax.all_gather(shard_set[4], "shard", axis=0, tiled=True),
        lax.all_gather(shard_set[5], "shard", axis=0, tiled=True),
        lax.all_gather(shard_set[6], "shard", axis=0, tiled=True),
        lax.all_gather(shard_set[7], "shard", axis=0, tiled=True),
        lax.all_gather(shard_set[8], "shard", axis=0, tiled=True),
        lax.all_gather(shard_set[9], "shard", axis=0, tiled=True),
        lax.all_gather(shard_set[10], "shard", axis=0, tiled=True),
        lax.all_gather(shard_set[11], "shard", axis=0, tiled=True),
        lax.all_gather(shard_set[12], "shard", axis=0, tiled=True),
    )
    d_input, grads = layer_backward(upstream, key_mask, again, stored, images)
    reduced = reduce_grads(grads)
    input_grad = d_input.astype(jnp.bfloat16).reshape(images, tok_local, D)
    return (
        output,
        input_grad,
        reduced[0],
        reduced[1],
        reduced[2],
        reduced[3],
        reduced[4],
        reduced[5],
        reduced[6],
        reduced[7],
        reduced[8],
        reduced[9],
        reduced[10],
        reduced[11],
        reduced[12],
    )


def solution(mesh):
    in_specs = (
        P("shard", "seq", None),
        P("shard", None),
        P("shard", "seq", None),
        P("shard"),
        P("shard"),
        P("shard", None),
        P("shard"),
        P("shard"),
        P("shard", None),
        P("shard"),
        P("shard"),
        P("shard"),
        P("shard", None),
        P("shard"),
        P("shard", None),
        P("shard"),
    )
    out_specs = (
        P("shard", "seq", None),
        P("shard", "seq", None),
        P("shard"),
        P("shard"),
        P("shard", None),
        P("shard"),
        P("shard"),
        P("shard", None),
        P("shard"),
        P("shard"),
        P("shard"),
        P("shard", None),
        P("shard"),
        P("shard", None),
        P("shard"),
    )
    return jax.shard_map(
        per_device, mesh=mesh, in_specs=in_specs, out_specs=out_specs, check_vma=False
    )
```

profile of v0, /device:TPU:1, one launch (start us, length us, event | category | flops | bytes accessed | tf_op | source)
XLA Modules:
  0.0 1049.5 jit_solution(10509725914430897723)
XLA Ops:
  10.7 17.9 %all-gather.3 = bf16[8,1,128]{2,1,0:T(2,128)(2,1)S(1)} all-gather(bf16[1,1,128]{2,1,0:T(2,128)(2,1)S(1)} %bitcast.126), channel_id=1, replica_groups=mesh['seq'=4,'shard'=8] {'shard'}, dimensions={0}, use_global_device_ids=true | all-gather | bytes 2304 | tf_op jit(solution)/shard_map/all_gather | solution.py:337
  28.5 12.9 %all-gather.2 = bf16[8,1,128]{2,1,0:T(2,128)(2,1)S(1)} all-gather(bf16[1,1,128]{2,1,0:T(2,128)(2,1)S(1)} %bitcast.127), channel_id=1, replica_groups=mesh['seq'=4,'shard'=8] {'shard'}, dimensions={0}, use_global_device_ids=true | all-gather | bytes 2304 | tf_op jit(solution)/shard_map/all_gather | solution.py:336
  41.5 15.1 %all-gather.1 = bf16[8,1,128]{2,1,0:T(2,128)(2,1)S(1)} all-gather(bf16[1,1,128]{2,1,0:T(2,128)(2,1)S(1)} %bitcast.128), channel_id=1, replica_groups=mesh['seq'=4,'shard'=8] {'shard'}, dimensions={0}, use_global_device_ids=true | all-gather | bytes 2304 | tf_op jit(solution)/shard_map/all_gather | solution.py:334
  56.5 13.0 %all-gather = bf16[8,1,128]{2,1,0:T(2,128)(2,1)S(1)} all-gather(bf16[1,1,128]{2,1,0:T(2,128)(2,1)S(1)} %bitcast.129), channel_id=1, replica_groups=mesh['seq'=4,'shard'=8] {'shard'}, dimensions={0}, use_global_device_ids=true | all-gather | bytes 2304 | tf_op jit(solution)/shard_map/all_gather | solution.py:333
  71.4 39.6 %all-gather.14.cloned.1.call-done = bf16[1024,3072]{1,0:T(8,128)(2,1)} async-done(((bf16[128,3072]{1,0:T(8,128)(2,1)}), bf16[1024,3072]{1,0:T(8,128)(2,1)}) %all-gather.14.cloned.1.call-update) | async-done | bytes 6291472 | tf_op jit(solution)/shard_map/all_gather | solution.py:335
  122.5 8.2 copy.128
  135.7 36.1 %all-to-all-done = bf16[2,146,3,1024]{1,0,2,3:T(2,128)(2,1)S(1)} async-done(((bf16[2,146,3,1024]{1,0,2,3:T(2,128)(2,1)}), bf16[2,146,3,1024]{1,0,2,3:T(2,128)(2,1)S(1)}, u32[]{:S(2)}, u32[]{:S(2)}) %all-to-all-start) | async-done | bytes 1794080 | tf_op jit(solution)/shard_map/all_to_all | solution.py:89
  203.4 13.9 %all-gather.4 = bf16[8,1,128]{2,1,0:T(2,128)(2,1)S(1)} all-gather(bf16[1,1,128]{2,1,0:T(2,128)(2,1)S(1)} %bitcast.130), channel_id=1, replica_groups=mesh['seq'=4,'shard'=8] {'shard'}, dimensions={0}, use_global_device_ids=true | all-gather | bytes 2304 | tf_op jit(solution)/shard_map/all_gather | solution.py:339
  217.4 22.9 %all-gather.7 = bf16[8,1,512]{2,1,0:T(2,128)(2,1)S(1)} all-gather(bf16[1,1,512]{2,1,0:T(2,128)(2,1)S(1)} %reshape.196), channel_id=1, replica_groups=mesh['seq'=4,'shard'=8] {'shard'}, dimensions={0}, use_global_device_ids=true | all-gather | bytes 9216 | tf_op jit(solution)/shard_map/all_gather | solution.py:343
  240.3 13.8 %all-gather.6 = bf16[8,1,128]{2,1,0:T(2,128)(2,1)S(1)} all-gather(bf16[1,1,128]{2,1,0:T(2,128)(2,1)S(1)} %bitcast.131), channel_id=1, replica_groups=mesh['seq'=4,'shard'=8] {'shard'}, dimensions={0}, use_global_device_ids=true | all-gather | bytes 2304 | tf_op jit(solution)/shard_map/all_gather | solution.py:341
  254.1 14.4 %all-gather.5 = bf16[8,1,128]{2,1,0:T(2,128)(2,1)S(1)} all-gather(bf16[1,1,128]{2,1,0:T(2,128)(2,1)S(1)} %bitcast.132), channel_id=1, replica_groups=mesh['seq'=4,'shard'=8] {'shard'}, dimensions={0}, use_global_device_ids=true | all-gather | bytes 2304 | tf_op jit(solution)/shard_map/all_gather | solution.py:340
  276.7 10.1 all-gather.18.cloned.1.call-done
  286.7 8.3 convolution_add_fusion
  295.1 116.8 %all-gather.20.cloned.1.call-done = bf16[4096,1024]{1,0:T(8,128)(2,1)} async-done(((bf16[512,1024]{1,0:T(8,128)(2,1)}), bf16[4096,1024]{1,0:T(8,128)(2,1)}) %all-gather.20.cloned.1.call-update) | async-done | bytes 8388624 | tf_op jit(solution)/shard_map/all_gather | solution.py:344
  411.9 9.1 fusion.32
  426.6 13.9 %convolution_convert_fusion.4 = bf16[292,1024]{1,0:T(8,128)(2,1)} fusion(bf16[1024,1024]{1,0:T(8,128)(2,1)S(1)} %copy-done.38, f32[292,1024]{1,0:T(8,128)S(1)} %get-tuple-element.123), kind=kOutput, calls=%fused_computation.36 | convolution fusion | flops 612966400 | bytes 3891200 | tf_op jit(solution)/shard_map/dot_general | solution.py:24
  455.1 10.0 all-to-all-done.2
  468.7 8.5 fusion.12
  477.2 9.2 multiply_reduce_fusion
  488.2 9.6 multiply_convert_fusion
  515.9 19.5 %all-to-all-done.3 = bf16[2,584,3,256]{3,0,2,1:T(2,128)(2,1)S(1)} async-done(((bf16[2,584,3,256]{3,0,2,1:T(2,128)(2,1)}), bf16[2,584,3,256]{3,0,2,1:T(2,128)(2,1)S(1)}, u32[]{:S(2)}, u32[]{:S(2)}) %all-to-all-start.3) | async-done | bytes 1794080 | tf_op jit(solution)/shard_map/all_to_all | solution.py:208
  538.7 7.1 convolution_convert_fusion.2
  547.1 8.7 convolution_convert_fusion.1
  557.1 9.5 convolution_convert_fusion
  567.3 14.6 %all-gather.8 = bf16[8,1,128]{2,1,0:T(2,128)(2,1)S(1)} all-gather(bf16[1,1,128]{2,1,0:T(2,128)(2,1)S(1)} %bitcast.133), channel_id=1, replica_groups=mesh['seq'=4,'shard'=8] {'shard'}, dimensions={0}, use_global_device_ids=true | all-gather | bytes 2304 | tf_op jit(solution)/shard_map/all_gather | solution.py:345
  584.5 7.8 fusion.17
  595.9 64.8 %reduce-scatter.5.cloned.1.call-done = bf16[128,3072]{1,0:T(8,128)(2,1)} async-done(((bf16[1024,3072]{1,0:T(8,128)(2,1)}), bf16[128,3072]{1,0:T(8,128)(2,1)}) %reduce-scatter.5.cloned.1.call-update) | async-done | bytes 786448 | tf_op jit(solution)/shard_map/reduce_scatter | solution.py:244
  660.7 152.6 %reduce-scatter.9.cloned.1.call-done = bf16[128,4096]{1,0:T(8,128)(2,1)} async-done(((bf16[1024,4096]{1,0:T(8,128)(2,1)}), bf16[128,4096]{1,0:T(8,128)(2,1)}) %reduce-scatter.9.cloned.1.call-update) | async-done | bytes 1048592 | tf_op jit(solution)/shard_map/reduce_scatter | solution.py:265
  813.3 152.1 %reduce-scatter.11.cloned.1.call-done = bf16[512,1024]{1,0:T(8,128)(2,1)} async-done(((bf16[4096,1024]{1,0:T(8,128)(2,1)}), bf16[512,1024]{1,0:T(8,128)(2,1)}) %reduce-scatter.11.cloned.1.call-update) | async-done | bytes 1048592 | tf_op jit(solution)/shard_map/reduce_scatter | solution.py:271
  975.2 28.0 %all-reduce.9 = (bf16[1024]{0:T(1024)(128)(2,1)S(1)}, bf16[1024]{0:T(1024)(128)(2,1)S(1)}, bf16[1024]{0:T(1024)(128)(2,1)S(1)}, bf16[1024]{0:T(1024)(128)(2,1)S(...) all-reduce(bf16[1024]{0:T(1024)(128)(2,1)S(1)} %get-tuple-element.9, ...), channel_id=2, replica_groups=mesh['seq'=4,'shard'=8] {'shard'}, use_global_device_ids=true, to_apply=%region_12.13.clone | all-reduce | flops 12288 | bytes 49152
  1003.8 12.9 %all-reduce.10 = (bf16[128]{0:T(256)(128)(2,1)S(1)}, bf16[128]{0:T(256)(128)(2,1)S(1)}, bf16[128]{0:T(256)(128)(2,1)S(1)}, bf16[128]{0:T(256)(128)(2,1)S(1)}, bf...) all-reduce(bf16[128]{0:T(256)(128)(2,1)S(1)} %dynamic-slice.1, ...), channel_id=1, replica_groups=mesh['seq'=4,'shard'=8] {'seq'}, use_global_device_ids=true, to_apply=%region_13.14 | all-reduce | flops 1536 | bytes 6144 | tf_op jit(solution)/shard_map/psum | solution.py:279
  1021.4 14.7 %all-reduce.14.cloned.1.call-done = (bf16[128,3072]{1,0:T(8,128)(2,1)}, bf16[128,1024]{1,0:T(8,128)(2,1)}, bf16[128,4096]{1,0:T(8,128)(2,1)}, bf16[512,1024]{1,0:T(8,128)(2,1)}) async-done(((bf16[128,3072]{1,0:T(8,128)(2,1)}, bf16[128,1024]{1,0:T(8,128)(2,1)}, bf16[128,4096]{1,0:T(8,128)(2,1)}, bf16[512,1024]{1,0:T(8,128)(2,1)}), (bf16[128,3072]{1,0:T(8,128)(2,1)}, bf16[128,1024]{1,0:T(8,128)(2,1)}, ...) | async-done | bytes 3145744 | tf_op jit(solution)/shard_map/psum | solution.py:281
  (210 shorter events, 137.9 us)
Async XLA Ops:
  7.2 103.8 %all-gather.14.cloned.1.call-start = ((), (), s32[]{:S(2)}) async-start(), calls=%async_computation.8 | async-start | bytes 7077888 | tf_op jit(solution)/shard_map/all_gather | solution.py:335
  7.9 265.4 %all-gather.16.cloned.1.call-start = ((), (), s32[]{:S(2)}) async-start(), calls=%async_computation.9 | async-start | bytes 2359296 | tf_op jit(solution)/shard_map/all_gather | solution.py:338
  8.7 278.1 %all-gather.18.cloned.1.call-start = ((), (), s32[]{:S(2)}) async-start(), calls=%async_computation.10 | async-start | bytes 9437184 | tf_op jit(solution)/shard_map/all_gather | solution.py:342
  9.4 402.5 %all-gather.20.cloned.1.call-start = ((), (), s32[]{:S(2)}) async-start(), calls=%async_computation.11 | async-start | bytes 9437184 | tf_op jit(solution)/shard_map/all_gather | solution.py:344
  10.0 18.5 %copy-start.30 = (bf16[128]{0:T(256)(128)(2,1)S(1)}, bf16[128]{0:T(256)(128)(2,1)}, u32[]{:S(2)}) copy-start(bf16[128]{0:T(256)(128)(2,1)} %param.22) | copy-start | bytes 772
  10.0 31.4 %copy-start.31 = (bf16[128]{0:T(256)(128)(2,1)S(1)}, bf16[128]{0:T(256)(128)(2,1)}, u32[]{:S(2)}) copy-start(bf16[128]{0:T(256)(128)(2,1)} %param.20) | copy-start | bytes 772
  10.0 46.5 %copy-start.32 = (bf16[128]{0:T(256)(128)(2,1)S(1)}, bf16[128]{0:T(256)(128)(2,1)}, u32[]{:S(2)}) copy-start(bf16[128]{0:T(256)(128)(2,1)} %param.19) | copy-start | bytes 772
  10.3 100.7 %copy-start.11 = (f32[292,1024]{1,0:T(8,128)}, f32[292,1024]{1,0:T(8,128)S(1)}, u32[]{:S(2)}) copy-start(f32[292,1024]{1,0:T(8,128)S(1)} %reshape.173) | copy-start | bytes 3588100
  71.3 45.9 %copy-start.21 = (f32[292]{0:T(512)}, f32[292]{0:T(512)S(1)}, u32[]{:S(2)}) copy-start(f32[292]{0:T(512)S(1)} %rsqrt.21) | copy-start | bytes 3508
  71.4 45.8 %copy-start.23 = (f32[292]{0:T(512)}, f32[292]{0:T(512)S(1)}, u32[]{:S(2)}) copy-start(f32[292]{0:T(512)S(1)} %div.39) | copy-start | bytes 3508
  130.8 41.0 %all-to-all-start = ((bf16[2,146,3,1024]{1,0,2,3:T(2,128)(2,1)}), bf16[2,146,3,1024]{1,0,2,3:T(2,128)(2,1)S(1)}, u32[]{:S(2)}, u32[]{:S(2)}) async-start(bf16[2,146,3,1024]{1,0,2,3:T(2,128)(2,1)} %copy.128), calls=%async_computation | async-start | bytes 6291456 | tf_op jit(solution)/shard_map/all_to_all | solution.py:89
  196.2 21.2 %copy-start.28 = (bf16[512]{0:T(512)(128)(2,1)S(1)}, bf16[512]{0:T(512)(128)(2,1)}, u32[]{:S(2)}) copy-start(bf16[512]{0:T(512)(128)(2,1)} %param.29) | copy-start | bytes 3076
  196.2 44.1 %copy-start.34 = (bf16[128]{0:T(256)(128)(2,1)S(1)}, bf16[128]{0:T(256)(128)(2,1)}, u32[]{:S(2)}) copy-start(bf16[128]{0:T(256)(128)(2,1)} %param.27) | copy-start | bytes 772
  196.2 57.9 %copy-start.35 = (bf16[128]{0:T(256)(128)(2,1)S(1)}, bf16[128]{0:T(256)(128)(2,1)}, u32[]{:S(2)}) copy-start(bf16[128]{0:T(256)(128)(2,1)} %param.26) | copy-start | bytes 772
  196.2 72.5 %copy-start.14 = (bf16[2,146,1024]{2,0,1:T(2,128)(2,1)S(1)}, bf16[2,146,1024]{2,0,1:T(2,128)(2,1)}, u32[]{:S(2)}) copy-start(bf16[2,146,1024]{2,0,1:T(2,128)(2,1)} %param.18) | copy-start | bytes 1794052
  198.4 72.4 %all-to-all-start.1 = ((bf16[2,584,256]{2,0,1:T(2,128)(2,1)}), bf16[2,584,256]{2,0,1:T(2,128)(2,1)}, u32[]{:S(2)}, u32[]{:S(2)}) async-start(bf16[2,584,256]{2,0,1:T(2,128)(2,1)} %copy.135), calls=%async_computation.1 | async-start | bytes 1196032 | tf_op jit(solution)/shard_map/all_to_all | solution.py:107
  254.1 32.6 %copy-start.25 = (f32[8,1,128]{2,1,0:T(1,128)}, f32[8,1,128]{2,1,0:T(1,128)S(1)}, u32[]{:S(2)}) copy-start(f32[8,1,128]{2,1,0:T(1,128)S(1)} %convert_element_type.253) | copy-start | bytes 12292
  276.4 144.7 %copy-start.7 = (f32[292,1024]{1,0:T(8,128)}, f32[292,1024]{1,0:T(8,128)S(1)}, u32[]{:S(2)}) copy-start(f32[292,1024]{1,0:T(8,128)S(1)} %get-tuple-element.130) | copy-start | bytes 3588100
  426.5 24.9 %copy-start.5 = (f32[292,1024]{1,0:T(8,128)}, f32[292,1024]{1,0:T(8,128)S(1)}, u32[]{:S(2)}) copy-start(f32[292,1024]{1,0:T(8,128)S(1)} %get-tuple-element.123) | copy-start | bytes 3588100
  446.1 19.0 %all-to-all-start.2 = ((bf16[2,146,1024]{1,0,2:T(2,128)(2,1)}), bf16[2,146,1024]{1,0,2:T(2,128)(2,1)}, u32[]{:S(2)}, u32[]{:S(2)}) async-start(bf16[2,146,1024]{1,0,2:T(2,128)(2,1)} %copy.140), calls=%async_computation.2 | async-start | bytes 2097152 | tf_op jit(solution)/shard_map/all_to_all | solution.py:183
  451.4 144.5 %reduce-scatter.7.cloned.1.call-start = ((), (), s32[]{:S(2)}) async-start(), calls=%async_computation.13 | async-start | bytes 2359296 | tf_op jit(solution)/shard_map/reduce_scatter | solution.py:253
  509.4 26.0 %all-to-all-start.3 = ((bf16[2,584,3,256]{3,0,2,1:T(2,128)(2,1)}), bf16[2,584,3,256]{3,0,2,1:T(2,128)(2,1)S(1)}, u32[]{:S(2)}, u32[]{:S(2)}) async-start(bf16[2,584,3,256]{3,0,2,1:T(2,128)(2,1)} %pad_maximum_fusion), calls=%async_computation.3 | async-start | bytes 3588096 | tf_op jit(solution)/shard_map/all_to_all | solution.py:208
  513.8 146.9 %reduce-scatter.5.cloned.1.call-start = ((), (), s32[]{:S(2)}) async-start(), calls=%async_computation.12 | async-start | bytes 7077888 | tf_op jit(solution)/shard_map/reduce_scatter | solution.py:244
  545.8 267.5 %reduce-scatter.9.cloned.1.call-start = ((), (), s32[]{:S(2)}) async-start(), calls=%async_computation.14 | async-start | bytes 9437184 | tf_op jit(solution)/shard_map/reduce_scatter | solution.py:265
  555.8 409.5 %reduce-scatter.11.cloned.1.call-start = ((), (), s32[]{:S(2)}) async-start(), calls=%async_computation.15 | async-start | bytes 9437184 | tf_op jit(solution)/shard_map/reduce_scatter | solution.py:271
  566.6 15.3 %copy-start.39 = (u32[32]{0:T(128)S(1)}, u32[32]{0:T(128)}, u32[]{:S(2)}) copy-start(u32[32]{0:T(128)} %constant.49) | copy-start | bytes 388
  566.6 17.1 %copy-start.15 = (bf16[2,146,1024]{2,0,1:T(2,128)(2,1)S(1)}, bf16[2,146,1024]{2,0,1:T(2,128)(2,1)}, u32[]{:S(2)}) copy-start(bf16[2,146,1024]{2,0,1:T(2,128)(2,1)} %param.18) | copy-start | bytes 1794052
  566.7 469.4 %all-reduce.14.cloned.1.call-start = ((), (), s32[]{:S(2)}) async-start(), calls=%async_computation.16 | async-start | bytes 6291456 | tf_op jit(solution)/shard_map/psum | solution.py:281
  593.2 372.2 %copy-start.4 = (bf16[292,3072]{1,0:T(8,128)(2,1)S(1)}, bf16[292,3072]{1,0:T(8,128)(2,1)}, u32[]{:S(2)}) copy-start(bf16[292,3072]{1,0:T(8,128)(2,1)} %reshape.180) | copy-start | bytes 5382148
  593.2 372.2 %copy-start.12 = (f32[292,1024]{1,0:T(8,128)S(1)}, f32[292,1024]{1,0:T(8,128)}, u32[]{:S(2)}) copy-start(f32[292,1024]{1,0:T(8,128)} %copy-done.11) | copy-start | bytes 3588100
  593.2 372.2 %copy-start.22 = (f32[292]{0:T(512)S(1)}, f32[292]{0:T(512)}, u32[]{:S(2)}) copy-start(f32[292]{0:T(512)} %copy-done.21) | copy-start | bytes 3508
  593.2 372.2 %copy-start.24 = (f32[292]{0:T(512)S(1)}, f32[292]{0:T(512)}, u32[]{:S(2)}) copy-start(f32[292]{0:T(512)} %copy-done.23) | copy-start | bytes 3508
  (22 other events, 77.6 us)
Sparse Core Ops, SparseCore 0:
  10.2 100.7 all-gather.13
  113.1 46.8 all-gather.15
  162.2 124.5 all-gather.17
  288.7 123.1 all-gather.19
  456.0 64.5 reduce-scatter.6
  545.9 114.6 reduce-scatter.4
  664.3 148.9 reduce-scatter.8
  817.3 147.9 reduce-scatter.10
  968.0 68.0 all-reduce.13
where the time goes:
time: 1060 us; the launch traced here: 1050 us
  waiting for transfers between devices  619 us (58%)
  blocking collectives  179 us (17%)
  matrix products  117 us (11%)
  local copies, waits for them, and re-layouts  63.6 us (6%)
  other arithmetic  34.7 us (3%)
  starting transfers between devices  20 us (2%)
  between operations  16.2 us (2%)
    reduce_scatter x1, waiting for transfers between devices, reduce_grads(): lax.psum_scatter(grads[9].astype(jnp.bfloat16), 'shard', scatter_dimensio...  153 us
    reduce_scatter x1, waiting for transfers between devices, reduce_grads(): lax.psum_scatter(grads[11].astype(jnp.bfloat16), 'shard', scatter_dimensi...  152 us
    all_gather x1, waiting for transfers between devices, per_device(): lax.all_gather(shard_set[11], 'shard', axis=0, tiled=True)  117 us
    reduce_scatter x1, waiting for transfers between devices, reduce_grads(): lax.psum_scatter(grads[2].astype(jnp.bfloat16), 'shard', scatter_dimensio...  64.8 us
    all_gather x1, waiting for transfers between devices, per_device(): lax.all_gather(shard_set[2], 'shard', axis=0, tiled=True)  39.6 us
    all_to_all x1, waiting for transfers between devices, layer_forward(): lax.all_to_all(packed, 'seq', split_axis=3, concat_axis=1, tiled=True)  36.1 us
    dot_general x4, matrix products, product_nt(): lax.dot_general(left, right, (((1,), (1,)), ((), ())), preferred_element_...  31.9 us
    dot_general x4, matrix products, product_tn(): lax.dot_general(left, right, (((0,), (0,)), ((), ())), preferred_element_...  29 us
  transfers between devices with their start and end apart: 13, of which 10 were waited for; matrix products, arithmetic and copies ran while one was open for 16% of the time, Pallas kernels for 0%

commit v1 on v0

--- a/solution.py
+++ b/solution.py
@@ -1,6 +1,8 @@
 import jax
 import jax.numpy as jnp
 from jax import lax
+from jax.experimental import pallas as pl
+from jax.experimental.pallas import tpu as pltpu
 from jax.sharding import PartitionSpec as P
 
 D = 1024
@@ -386,6 +388,699 @@
     )
 
 
+NSEQ = 4
+NSH = 8
+TOK = 160
+ROWS = NSEQ * TOK
+HEADS_DEV = 4
+MASKED = -1e30
+VMEM_LIMIT = 64 * 1024 * 1024 - 1024 * 1024
+MESH_ID = pl.DeviceIdType.MESH
+BF = jnp.bfloat16
+F32 = jnp.float32
+GATE = 1.702
+
+
+def dot_nn(left, right):
+    return lax.dot_general(left, right, (((1,), (0,)), ((), ())), preferred_element_type=F32)
+
+
+def dot_nt(left, right):
+    return lax.dot_general(left, right, (((1,), (1,)), ((), ())), preferred_element_type=F32)
+
+
+def dot_tn(left, right):
+    return lax.dot_general(left, right, (((0,), (0,)), ((), ())), preferred_element_type=F32)
+
+
+def layer_kernel(
+    xin, dmin, bias, pack, wq_h, wo_h, wu_h, wd_h,
+    out_o, dx_o, gq_o, go_o, gu_o, gd_o, sg_o,
+    xg, wq, wo, wu, wd, pg, qkv, dqkv, probs, mixt, mixed, part, rc, rx, rc2, rx2,
+    hid, cg, act, gate, dmg, dhid, dmix,
+    gq, go, gu, gd, ryq, ryo, ryu, ryd, rzq, rzo, rzu, rzd, sgs, sg1, sg2,
+    ssem, rsem, lsem,
+):
+    s = lax.axis_index("seq")
+    j = lax.axis_index("shard")
+    x, k = s // 2, s % 2
+    z, y = j // 2, j % 2
+    s_core = x * 2 + (1 - k)
+    s_x = (1 - x) * 2 + k
+    s_diag = (1 - x) * 2 + (1 - k)
+    j_y = z * 2 + (1 - y)
+    core = (s_core, j)
+    xdev = (s_x, j)
+    ydev = (s, j_y)
+
+    def zj(d):
+        return lax.rem(z + d, 4) * 2 + y
+
+    ids = {}
+
+    def ix(*key):
+        return ids.setdefault(key, len(ids))
+
+    pending = {}
+
+    def send(tag, key, src, dst, dev):
+        n = ix(*key)
+        copy = pltpu.make_async_remote_copy(
+            src_ref=src, dst_ref=dst, send_sem=ssem.at[n], recv_sem=rsem.at[n],
+            device_id=dev, device_id_type=MESH_ID)
+        copy.start()
+        pending.setdefault(tag, []).append(copy)
+
+    def sent(tag):
+        for copy in pending.pop(tag, []):
+            copy.wait_send()
+
+    def arrived(key, dst, dev):
+        n = ix(*key)
+        pltpu.make_async_remote_copy(
+            src_ref=dst, dst_ref=dst, send_sem=ssem.at[n], recv_sem=rsem.at[n],
+            device_id=dev, device_id_type=MESH_ID).wait_recv()
+
+    local = {}
+
+    def load(key, src, dst):
+        copy = pltpu.make_async_copy(src, dst, lsem.at[local.setdefault(key, len(local))])
+        copy.start()
+        return copy
+
+    def rows(block):
+        return pl.ds(pl.multiple_of(block * TOK, TOK), TOK)
+
+    def tiles(count, step, body, init=None):
+        def inner(t, carry):
+            return body(pl.multiple_of(t * step, step), carry)
+        return lax.fori_loop(0, count // step, inner, init)
+
+    barrier = pltpu.get_barrier_semaphore()
+    for d in range(1, NSEQ):
+        pl.semaphore_signal(barrier, inc=1, device_id=(lax.rem(s + d, NSEQ), j), device_id_type=MESH_ID)
+    for d in range(1, NSH):
+        pl.semaphore_signal(barrier, inc=1, device_id=(s, lax.rem(j + d, NSH)), device_id_type=MESH_ID)
+    loads_q = [load(("wq", c), wq_h.at[:, pl.ds(pl.multiple_of(1024 * c + 256 * s, 256), 256)],
+                    wq.at[j, :, pl.ds(256 * c, 256)]) for c in range(3)]
+    loads_u = [load(("wu", c), wu_h.at[:, pl.ds(pl.multiple_of(512 * c + 128 * s, 128), 128)],
+                    wu.at[j, :, pl.ds(128 * c, 128)]) for c in range(8)]
+    load_d = load(("wd",), wd_h.at[pl.ds(pl.multiple_of(128 * s, 128), 128)], wd.at[j])
+    pg[j] = pack[...]
+    pl.semaphore_wait(barrier, NSEQ - 1 + NSH - 1)
+
+    def ag4_start(key, buf, i, src):
+        send(key, (key, "c", i), src, buf.at[i, rows(s)], core)
+        send(key, (key, "x", i), src, buf.at[i, rows(s)], xdev)
+
+    def ag4_forward(key, buf, i):
+        arrived((key, "x", i), buf.at[i, rows(s_x)], xdev)
+        send(key + "f", (key, "d", i), buf.at[i, rows(s_x)], buf.at[i, rows(s_x)], core)
+
+    def ag4_end(key, buf, i):
+        arrived((key, "c", i), buf.at[i, rows(s_core)], core)
+        arrived((key, "d", i), buf.at[i, rows(s_diag)], core)
+
+    def agw_start(key, buf):
+        send(key, (key, "y", 0), buf.at[j], buf.at[j], ydev)
+        for d in (1, 2, 3):
+            send(key, (key, "z", d), buf.at[j], buf.at[j], (s, zj(d)))
+
+    def agw_forward(key, buf, d):
+        jf = zj(4 - d)
+        arrived((key, "z", d), buf.at[jf], (s, jf))
+        send(key, (key, "y", d), buf.at[jf], buf.at[jf], ydev)
+
+    def agw_end(key, buf):
+        for d in (0, 1, 2, 3):
+            jf = lax.rem(z + 4 - d, 4) * 2 + (1 - y)
+            arrived((key, "y", d), buf.at[jf], ydev)
+
+    def rs4_a(key, i, rcb):
+        send(key, (key, "c0", i), part.at[i, rows(s_core)], rcb.at[i, 0], core)
+        send(key, (key, "c1", i), part.at[i, rows(s_diag)], rcb.at[i, 1], core)
+
+    def rs4_b(key, i, rcb, rxb):
+        arrived((key, "c1", i), rcb.at[i, 1], core)
+
+        def add(r, _):
+            here = pl.ds(pl.multiple_of(s_x * TOK + r, 32), 32)
+            total = part[i, here, :].astype(F32) + rcb[i, 1, pl.ds(r, 32), :].astype(F32)
+            part[i, here, :] = total.astype(BF)
+        tiles(TOK, 32, add)
+        send(key, (key, "x", i), part.at[i, rows(s_x)], rxb.at[i], xdev)
+
+    def rs4_wait(key, i, rcb, rxb):
+        arrived((key, "c0", i), rcb.at[i, 0], core)
+        arrived((key, "x", i), rxb.at[i], xdev)
+
+    def rs4_sum(i, r, rcb, rxb):
+        here = pl.ds(pl.multiple_of(s * TOK + r, 32), 32)
+        return (part[i, here, :].astype(F32) + rcb[i, 0, pl.ds(r, 32), :].astype(F32)
+                + rxb[i, pl.ds(r, 32), :].astype(F32))
+
+    def add_into(g, row, others):
+        def add(r, _):
+            total = g[row, pl.ds(r, 32), :].astype(F32)
+            for ref, at in others:
+                total = total + ref[at, pl.ds(r, 32), :].astype(F32)
+            g[row, pl.ds(r, 32), :] = total.astype(BF)
+        tiles(128, 32, add)
+
+    def rsw_start(key, g, ry):
+        for d in (1, 2, 3, 0):
+            send(key, (key, "gy", d), g.at[lax.rem(z + d, 4) * 2 + (1 - y)], ry.at[d], ydev)
+
+    def rsw_mid(key, g, ry, rz):
+        for d in (1, 2, 3, 0):
+            arrived((key, "gy", d), ry.at[d], ydev)
+            add_into(g, zj(d), [(ry, d)])
+            if d:
+                send(key, (key, "gz", d), g.at[zj(d)], rz.at[d - 1], (s, zj(d)))
+
+    def rsw_end(key, g, rz, g_o):
+        for d in (1, 2, 3):
+            arrived((key, "gz", d), rz.at[d - 1], (s, zj(4 - d)))
+        add_into(g, j, [(rz, 0), (rz, 1), (rz, 2)])
+        copy = load((key, "go"), g.at[j], g_o.at[s])
+        send(key, (key, "gc"), g.at[j], g_o.at[s], core)
+        send(key, (key, "gx"), g.at[j], g_o.at[s], xdev)
+        return copy
+
+    def rsw_forward(key, g_o):
+        arrived((key, "gx"), g_o.at[s_x], xdev)
+        send(key, (key, "gd"), g_o.at[s_x], g_o.at[s_x], core)
+
+    def rsw_done(key, g_o):
+        arrived((key, "gc"), g_o.at[s_core], core)
+        arrived((key, "gd"), g_o.at[s_diag], core)
+
+    def param(p):
+        return jnp.concatenate([pg[b, pl.ds(p, 1), :] for b in range(NSH)], axis=1)
+
+    def head_param(p):
+        return jnp.concatenate([pg[2 * s, pl.ds(p, 1), :], pg[2 * s + 1, pl.ds(p, 1), :]], axis=1)
+
+    def normal(value):
+        centre = jnp.mean(value, axis=-1, keepdims=True)
+        centred = value - centre
+        inverse = lax.rsqrt(jnp.mean(centred * centred, axis=-1, keepdims=True) + EPSILON)
+        return centred * inverse, inverse
+
+    def normal_back(incoming, scaled, inverse, gain):
+        inner = incoming * gain
+        return inverse * (inner - jnp.mean(inner, axis=-1, keepdims=True)
+                          - scaled * jnp.mean(inner * scaled, axis=-1, keepdims=True))
+
+    def fold(value):
+        return value[0:8] + value[8:16] + value[16:24] + value[24:32]
+
+    for i in range(2):
+        ag4_start("xg", xg, i, xin.at[i])
+    for d in range(1, NSH):
+        send("pk", ("pk", d), pack, pg.at[j], (s, lax.rem(j + d, NSH)))
+    for copy in loads_q:
+        copy.wait()
+    agw_start("wq", wq)
+    for i in range(2):
+        xg[i, rows(s), :] = xin[i]
+        dmg[i, rows(s), :] = dmin[i]
+    for d in range(1, NSH):
+        jf = lax.rem(j + NSH - d, NSH)
+        arrived(("pk", d), pg.at[jf], (s, jf))
+
+    attn_gain, attn_shift = param(0), param(1)
+
+    def norm_block(i, block):
+        def body(r, _):
+            here = pl.ds(pl.multiple_of(block * TOK + r, 32), 32)
+            scaled, _inverse = normal(xg[i, here, :].astype(F32))
+            xg[i, here, :] = (scaled * attn_gain + attn_shift).astype(BF)
+        tiles(TOK, 32, body)
+
+    norm_block(0, s)
+    norm_block(1, s)
+    ag4_forward("xg", xg, 0)
+    agw_forward("wq", wq, 1)
+    agw_forward("wq", wq, 2)
+    ag4_forward("xg", xg, 1)
+    agw_forward("wq", wq, 3)
+    for copy in loads_u:
+        copy.wait()
+    load_d.wait()
+
+    n_oz = [ix("woz", d) for d in (1, 2, 3)]
+
+    def out_copy(d):
+        return pltpu.make_async_remote_copy(
+            src_ref=wo.at[y], dst_ref=wo.at[y], send_sem=ssem.at[n_oz[d - 1]], recv_sem=rsem.at[n_oz[0]],
+            device_id=(s, zj(d)), device_id_type=MESH_ID)
+
+    @pl.when(z == s)
+    def _():
+        copy = pltpu.make_async_copy(wo_h, wo.at[y], lsem.at[local.setdefault("wo", len(local))])
+        copy.start()
+        copy.wait()
+        for d in (1, 2, 3):
+            out_copy(d).start()
+
+    agw_start("wu", wu)
+
+    for i in range(2):
+        ag4_end("xg", xg, i)
+        sent("xgf")
+        norm_block(i, s_core)
+        norm_block(i, s_x)
+        norm_block(i, s_diag)
+    for i in range(2):
+        ag4_start("dm", dmg, i, dmin.at[i])
+    agw_end("wq", wq)
+
+    @pl.when(z != s)
+    def _():
+        pltpu.make_async_remote_copy(
+            src_ref=wo.at[y], dst_ref=wo.at[y], send_sem=ssem.at[n_oz[0]], recv_sem=rsem.at[n_oz[0]],
+            device_id=(s, zj(1)), device_id_type=MESH_ID).wait_recv()
+    send("wo", ("wo", "y"), wo.at[y], wo.at[y], ydev)
+
+    packed_bias = jnp.concatenate([head_param(2), jnp.zeros((1, 256), F32), head_param(3)], axis=1)
+
+    def attend(i):
+        def project(r, _):
+            here = pl.ds(r, 320)
+            value = dot_nn(xg[i, here, :], wq[...].reshape(D, 768)) + packed_bias
+            qkv[i, here, :] = value.astype(BF)
+        tiles(ROWS, 320, project)
+        value_t = qkv[i, :, 512:768].astype(F32).T.astype(BF)
+        mixt[...] = value_t
+        lane = lax.broadcasted_iota(jnp.int32, (1, 256), 1) // HEAD_DIM
+
+        def one_head(h, _):
+            keyed = jnp.where(lane == h, qkv[i, :, 256:512], jnp.zeros((), BF))
+            query = qkv[i, :, 0:256] * jnp.asarray(HEAD_DIM ** -0.5, BF)
+            scores = dot_nt(keyed, query) + bias[i, :, 0:1]
+            raised = jnp.exp(scores - jnp.max(scores, axis=0, keepdims=True))
+            chances = (raised * (1.0 / jnp.sum(raised, axis=0, keepdims=True))).astype(BF)
+            probs[i, h] = chances
+            here = pl.ds(pl.multiple_of(h * HEAD_DIM, HEAD_DIM), HEAD_DIM)
+            mixt[here, :] = dot_nn(mixt[here, :], chances).astype(BF)
+        lax.fori_loop(0, HEADS_DEV, one_head, None)
+        mixed[i] = mixt[...].astype(F32).T.astype(BF)
+
+    def project_out(i):
+        def body(r, _):
+            here = pl.ds(r, 320)
+            part[i, here, :] = dot_nn(mixed[i, here, :], wo[...].reshape(256, D)).astype(BF)
+        tiles(ROWS, 320, body)
+
+    attend(0)
+    agw_forward("wu", wu, 1)
+    arrived(("wo", "y"), wo.at[1 - y], ydev)
+    project_out(0)
+    rs4_a("o", 0, rc)
+    agw_forward("wu", wu, 2)
+    agw_forward("wu", wu, 3)
+    agw_start("wd", wd)
+    rs4_b("o", 0, rc, rx)
+    attend(1)
+    project_out(1)
+    rs4_a("o", 1, rc)
+    rs4_b("o", 1, rc, rx)
+    for i in range(2):
+        ag4_forward("dm", dmg, i)
+
+    out_bias, mlp_gain, mlp_shift, down_bias = param(4), param(5), param(6), param(7)
+    up_bias = param(8)
+
+    for i in range(2):
+        rs4_wait("o", i, rc, rx)
+
+        def middle(r, _, i=i):
+            value = xin[i, pl.ds(r, 32), :].astype(F32) + (rs4_sum(i, r, rc, rx) + out_bias)
+            hid[i, pl.ds(r, 32), :] = value
+            scaled, _inverse = normal(value)
+            here = pl.ds(pl.multiple_of(s * TOK + r, 32), 32)
+            cg[i, here, :] = (scaled * mlp_gain + mlp_shift).astype(BF)
+        tiles(TOK, 32, middle)
+        ag4_start("c", cg, i, cg.at[i, rows(s)])
+    agw_forward("wd", wd, 1)
+    agw_forward("wd", wd, 2)
+    agw_forward("wd", wd, 3)
+    agw_end("wu", wu)
+    for i in range(2):
+        ag4_forward("c", cg, i)
+        if i == 0:
+            for n in range(2):
+                ag4_end("dm", dmg, n)
+        ag4_end("c", cg, i)
+
+        def up(r, _, i=i):
+            here = pl.ds(r, 320)
+            value = dot_nn(cg[i, here, :], wu[...].reshape(D, D)) + up_bias
+            sig = jax.nn.sigmoid(GATE * value)
+            act[i, here, :] = (value * sig).astype(BF)
+            gate[i, here, :] = (sig + GATE * value * sig * (1.0 - sig)).astype(BF)
+        tiles(ROWS, 320, up)
+    agw_end("wd", wd)
+    sent("o")
+
+    du_sum = jnp.zeros((8, D), F32)
+    for i in range(2):
+        def d_up(r, carry, i=i):
+            here = pl.ds(r, 320)
+            value = dot_nt(dmg[i, here, :], wd[...].reshape(D, D)) * gate[i, here, :].astype(F32)
+            value = value.astype(BF)
+            gate[i, here, :] = value
+            return carry + jnp.sum(value.astype(F32).reshape(40, 8, D), axis=0)
+        du_sum = tiles(ROWS, 320, d_up, du_sum)
+
+    def weight_grad(left, right, g):
+        def body(t, _):
+            cols = pl.ds(pl.multiple_of(t * 256, 256), 256)
+            value = dot_tn(left[:, :, cols].reshape(2 * ROWS, 256), right[...].reshape(2 * ROWS, right.shape[2]))
+            g[pl.ds(2 * t, 2)] = value.astype(BF).reshape(2, 128, right.shape[2])
+        lax.fori_loop(0, left.shape[2] // 256, body, None)
+
+    sent("dmf")
+    sent("dm")
+    weight_grad(act, dmg, gd)
+    rsw_start("d", gd, ryd)
+
+    def d_second(i):
+        def body(r, _):
+            here = pl.ds(r, 320)
+            part[i, here, :] = dot_nt(gate[i, here, :], wu[...].reshape(D, D)).astype(BF)
+        tiles(ROWS, 320, body)
+    for i in range(2):
+        d_second(i)
+        rs4_a("dc", i, rc)
+    rs4_b("dc", 0, rc, rx)
+    rs4_b("dc", 1, rc, rx)
+    weight_grad(cg, gate, gu)
+    rsw_start("u", gu, ryu)
+
+    zero8 = jnp.zeros((8, D), F32)
+    sums = (zero8, zero8, zero8, zero8)
+    for i in range(2):
+        rs4_wait("dc", i, rc, rx)
+
+        def d_middle(r, carry, i=i):
+            mine = pl.ds(r, 32)
+            incoming = rs4_sum(i, r, rc, rx)
+            scaled, inverse = normal(hid[i, mine, :])
+            upstream = dmin[i, mine, :].astype(F32)
+            value = upstream + normal_back(incoming, scaled, inverse, mlp_gain)
+            dhid[i, mine, :] = value
+            low = value.astype(BF)
+            dmg[i, pl.ds(pl.multiple_of(s * TOK + r, 32), 32), :] = low
+            return (carry[0] + fold(incoming * scaled), carry[1] + fold(incoming),
+                    carry[2] + fold(low.astype(F32)), carry[3] + fold(upstream))
+        sums = tiles(TOK, 32, d_middle, sums)
+        ag4_start("db", dmg, i, dmg.at[i, rows(s)])
+    sent("dc")
+
+    for i in range(2):
+        def down(r, _, i=i):
+            here = pl.ds(r, 320)
+            part[i, here, :] = dot_nn(act[i, here, :], wd[...].reshape(D, D)).astype(BF)
+        tiles(ROWS, 320, down)
+    rsw_mid("d", gd, ryd, rzd)
+    for i in range(2):
+        ag4_forward("db", dmg, i)
+    for i in range(2):
+        ag4_end("db", dmg, i)
+    for i in range(2):
+        rs4_a("y", i, rc2)
+
+    for i in range(2):
+        def d_mixed(r, _, i=i):
+            here = pl.ds(r, 320)
+            dmix[i, here, :] = dot_nt(dmg[i, here, :], wo[...].reshape(256, D)).astype(BF)
+        tiles(ROWS, 320, d_mixed)
+    value = dot_tn(mixed[...].reshape(2 * ROWS, 256), dmg[...].reshape(2 * ROWS, D))
+    go[...] = value.astype(BF).reshape(2, 128, D)
+    send("go", ("go", "y"), go.at[1 - y], ryo, ydev)
+    rs4_b("y", 0, rc2, rx2)
+    rs4_b("y", 1, rc2, rx2)
+
+    def attend_back(i):
+        lane = lax.broadcasted_iota(jnp.int32, (1, 256), 1) // HEAD_DIM
+        mixt[...] = qkv[i, :, 256:512].astype(F32).T.astype(BF)
+
+        def one_head(h, _):
+            own = lane == h
+            chances = probs[i, h]
+            d_value = dot_nn(chances, dmix[i])
+            dqkv[i, :, 512:768] = jnp.where(own, d_value.astype(BF), dqkv[i, :, 512:768])
+            valued = jnp.where(own, qkv[i, :, 512:768], jnp.zeros((), BF))
+            d_chances = dot_nt(valued, dmix[i])
+            wide = chances.astype(F32)
+            d_scores = wide * (d_chances - jnp.sum(wide * d_chances, axis=0, keepdims=True))
+            d_scores = d_scores.astype(BF)
+            d_key = dot_nn(d_scores, qkv[i, :, 0:256]) * HEAD_DIM ** -0.5
+            dqkv[i, :, 256:512] = jnp.where(own, d_key.astype(BF), dqkv[i, :, 256:512])
+            here = pl.ds(pl.multiple_of(h * HEAD_DIM, HEAD_DIM), HEAD_DIM)
+            mixt[here, :] = (dot_nn(mixt[here, :], d_scores) * HEAD_DIM ** -0.5).astype(BF)
+        lax.fori_loop(0, HEADS_DEV, one_head, None)
+        dqkv[i, :, 0:256] = mixt[...].astype(F32).T.astype(BF)
+
+    attend_back(0)
+    rsw_mid("u", gu, ryu, rzu)
+    copy_d = rsw_end("d", gd, rzd, gd_o)
+    arrived(("go", "y"), ryo, ydev)
+
+    def add_out(r, _):
+        total = go[y, pl.ds(r, 32), :].astype(F32) + ryo[pl.ds(r, 32), :].astype(F32)
+        go[y, pl.ds(r, 32), :] = total.astype(BF)
+    tiles(128, 32, add_out)
+    n_gz = [ix("goz", d) for d in range(3)]
+    n_gs = ix("gozs")
+
+    def out_grad_copy(slot):
+        return pltpu.make_async_remote_copy(
+            src_ref=go.at[y], dst_ref=rzo.at[slot], send_sem=ssem.at[n_gs], recv_sem=rsem.at[n_gz[0] + slot],
+            device_id=(s, s * 2 + y), device_id_type=MESH_ID)
+
+    @pl.when(z != s)
+    def _():
+        out_grad_copy(lax.rem(z + 3 - s, 4)).start()
+
+    attend_back(1)
+    sent("y")
+    for i in range(2):
+        rs4_wait("y", i, rc2, rx2)
+
+        def last(r, _, i=i):
+            mine = pl.ds(r, 32)
+            value = hid[i, mine, :] + (rs4_sum(i, r, rc2, rx2) + down_bias)
+            out_o[i, mine, :] = value.astype(BF)
+        tiles(TOK, 32, last)
+    for i in range(2):
+        def d_normed(r, _, i=i):
+            here = pl.ds(r, 320)
+            part[i, here, :] = dot_nt(dqkv[i, here, :], wq[...].reshape(D, 768)).astype(BF)
+        tiles(ROWS, 320, d_normed)
+        rs4_a("da", i, rc)
+    rs4_b("da", 0, rc, rx)
+    rs4_b("da", 1, rc, rx)
+    weight_grad(xg, dqkv, gq)
+    rsw_start("q", gq, ryq)
+
+    copy_u = rsw_end("u", gu, rzu, gu_o)
+
+    n_gb = [ix("gob", d) for d in range(3)]
+
+    def out_final_copy(d):
+        return pltpu.make_async_remote_copy(
+            src_ref=go.at[y], dst_ref=go_o, send_sem=ssem.at[n_gb[d - 1]], recv_sem=rsem.at[n_gb[0]],
+            device_id=(lax.rem(s + d, 4), j), device_id_type=MESH_ID)
+    n_ol = local.setdefault("go", len(local))
+
+    @pl.when(z == s)
+    def _():
+        for slot in range(3):
+            pltpu.make_async_remote_copy(
+                src_ref=go.at[y], dst_ref=rzo.at[slot], send_sem=ssem.at[n_gs], recv_sem=rsem.at[n_gz[slot]],
+                device_id=(s, zj(1)), device_id_type=MESH_ID).wait_recv()
+
+        def add(r, _):
+            total = go[y, pl.ds(r, 32), :].astype(F32)
+            for slot in range(3):
+                total = total + rzo[slot, pl.ds(r, 32), :].astype(F32)
+            go[y, pl.ds(r, 32), :] = total.astype(BF)
+        tiles(128, 32, add)
+        pltpu.make_async_copy(go.at[y], go_o, lsem.at[n_ol]).start()
+        for d in (1, 2, 3):
+            out_final_copy(d).start()
+    rsw_forward("d", gd_o)
+
+    sums_a = (zero8, zero8)
+    for i in range(2):
+        rs4_wait("da", i, rc, rx)
+
+        def d_input(r, carry, i=i):
+            mine = pl.ds(r, 32)
+            incoming = rs4_sum(i, r, rc, rx)
+            scaled, inverse = normal(xin[i, mine, :].astype(F32))
+            value = dhid[i, mine, :] + normal_back(incoming, scaled, inverse, attn_gain)
+            dx_o[i, mine, :] = value.astype(BF)
+            return carry[0] + fold(incoming * scaled), carry[1] + fold(incoming)
+        sums_a = tiles(TOK, 32, d_input, sums_a)
+
+    sgs[...] = jnp.zeros_like(sgs)
+
+    def place(row, total):
+        for b in range(NSH):
+            sgs[b, pl.ds(row, 1), :] = total[:, 128 * b:128 * b + 128]
+
+    def flat(value):
+        return jnp.sum(value, axis=0, keepdims=True)
+    place(0, flat(sums_a[0]))
+    place(1, flat(sums_a[1]))
+    place(4, flat(sums[2]))
+    place(5, flat(sums[0]))
+    place(6, flat(sums[1]))
+    place(7, flat(sums[3]))
+    d_query_sum = jnp.sum(dqkv[0, :, 0:256].astype(F32) + dqkv[1, :, 0:256].astype(F32), axis=0, keepdims=True)
+    d_value_sum = jnp.sum(dqkv[0, :, 512:768].astype(F32) + dqkv[1, :, 512:768].astype(F32), axis=0, keepdims=True)
+    for b in range(2):
+        sgs[2 * s + b, pl.ds(2, 1), :] = d_query_sum[:, 128 * b:128 * b + 128]
+        sgs[2 * s + b, pl.ds(3, 1), :] = d_value_sum[:, 128 * b:128 * b + 128]
+    up_sum = flat(du_sum)
+    row_at = lax.broadcasted_iota(jnp.int32, (8, 128), 0)
+    for b in range(NSH):
+        wide = jnp.broadcast_to(up_sum[:, 128 * b:128 * b + 128], (8, 128))
+        sgs[b, 8:16, :] = jnp.where(row_at == s, wide, 0.0)
+    for d in range(1, NSH):
+        send("sg", ("sg", d), sgs.at[lax.rem(j + d, NSH)], sg1.at[d - 1], (s, lax.rem(j + d, NSH)))
+
+    rsw_mid("q", gq, ryq, rzq)
+
+    for d in range(1, NSH):
+        jf = lax.rem(j + NSH - d, NSH)
+        arrived(("sg", d), sg1.at[d - 1], (s, jf))
+    total = sgs[j]
+    for d in range(1, NSH):
+        total = total + sg1[d - 1]
+    sg2[0] = total
+    for d in range(1, NSEQ):
+        send("sg", ("sh", d), sg2.at[0], sg2.at[d], (lax.rem(s + d, NSEQ), j))
+    rsw_forward("u", gu_o)
+    copy_q = rsw_end("q", gq, rzq, gq_o)
+    for d in range(1, NSEQ):
+        arrived(("sh", d), sg2.at[d], (lax.rem(s + NSEQ - d, NSEQ), j))
+    sg_o[...] = sg2[0] + sg2[1] + sg2[2] + sg2[3]
+    rsw_forward("q", gq_o)
+    rsw_done("d", gd_o)
+    rsw_done("u", gu_o)
+    rsw_done("q", gq_o)
+
+    @pl.when(z == s)
+    def _():
+        for d in (1, 2, 3):
+            out_final_copy(d).wait_send()
+            out_copy(d).wait_send()
+        pltpu.make_async_copy(go.at[y], go_o, lsem.at[n_ol]).wait()
+
+    @pl.when(z != s)
+    def _():
+        out_final_copy(1).wait_recv()
+        out_grad_copy(0).wait_send()
+    for copy in (copy_d, copy_u, copy_q):
+        copy.wait()
+    for tag in list(pending):
+        sent(tag)
+
+def fused_device(
+    inputs, key_mask, cotangent, attn_gain, attn_shift, qkv_weight, query_bias, value_bias,
+    out_weight, out_bias, mlp_gain, mlp_shift, up_weight, up_bias, down_weight, down_bias,
+):
+    tok = inputs.shape[1]
+    s = lax.axis_index("seq")
+    own_mask = lax.dynamic_slice_in_dim(key_mask, s * tok, tok, 1)
+    gap = ((0, 0), (0, TOK - tok), (0, 0))
+    xin = jnp.pad(inputs, gap)
+    dmin = jnp.pad(jnp.where(own_mask[:, :, None] > 0, cotangent, jnp.zeros((), BF)), gap)
+    slots = jnp.pad(key_mask.reshape(2, NSEQ, tok), ((0, 0), (0, 0), (0, TOK - tok)))
+    bias = jnp.where(slots.reshape(2, ROWS, 1) > 0, 0.0, MASKED)
+    bias = jnp.broadcast_to(bias, (2, ROWS, 128)).astype(F32)
+    own_up = lax.dynamic_slice_in_dim(up_bias, s * 128, 128, 0)
+    pack = jnp.stack(
+        (attn_gain, attn_shift, query_bias, value_bias, out_bias, mlp_gain, mlp_shift, down_bias, own_up)
+    ).astype(F32)
+    pack = jnp.pad(pack, ((0, 7), (0, 0)))
+    vm = pl.BlockSpec(memory_space=pltpu.VMEM)
+    hbm = pl.BlockSpec(memory_space=pl.ANY)
+
+    def shape(dims, dtype=BF):
+        return jax.ShapeDtypeStruct(dims, dtype)
+
+    outs = pl.pallas_call(
+        layer_kernel,
+        out_shape=(
+            shape((2, TOK, D)), shape((2, TOK, D)), shape((4, 128, 768)), shape((128, D)),
+            shape((4, 128, D)), shape((4, 128, D)), shape((16, 128), F32),
+        ),
+        in_specs=[vm, vm, vm, vm, hbm, hbm, hbm, hbm],
+        out_specs=(vm, vm, hbm, hbm, hbm, hbm, vm),
+        scratch_shapes=[
+            pltpu.VMEM((2, ROWS, D), BF),
+            pltpu.VMEM((8, 128, 768), BF),
+            pltpu.VMEM((2, 128, D), BF),
+            pltpu.VMEM((8, 128, D), BF),
+            pltpu.VMEM((8, 128, D), BF),
+            pltpu.VMEM((8, 16, 128), F32),
+            pltpu.VMEM((2, ROWS, 768), BF),
+            pltpu.VMEM((2, ROWS, 768), BF),
+            pltpu.VMEM((2, HEADS_DEV, ROWS, ROWS), BF),
+            pltpu.VMEM((256, ROWS), BF),
+            pltpu.VMEM((2, ROWS, 256), BF),
+            pltpu.VMEM((2, ROWS, D), BF),
+            pltpu.VMEM((2, 2, TOK, D), BF),
+            pltpu.VMEM((2, TOK, D), BF),
+            pltpu.VMEM((2, 2, TOK, D), BF),
+            pltpu.VMEM((2, TOK, D), BF),
+            pltpu.VMEM((2, TOK, D), F32),
+            pltpu.VMEM((2, ROWS, D), BF),
+            pltpu.VMEM((2, ROWS, D), BF),
+            pltpu.VMEM((2, ROWS, D), BF),
+            pltpu.VMEM((2, ROWS, D), BF),
+            pltpu.VMEM((2, TOK, D), F32),
+            pltpu.VMEM((2, ROWS, 256), BF),
+            pltpu.VMEM((8, 128, 768), BF),
+            pltpu.VMEM((2, 128, D), BF),
+            pltpu.VMEM((8, 128, D), BF),
+            pltpu.VMEM((8, 128, D), BF),
+            pltpu.VMEM((4, 128, 768), BF),
+            pltpu.VMEM((128, D), BF),
+            pltpu.VMEM((4, 128, D), BF),
+            pltpu.VMEM((4, 128, D), BF),
+            pltpu.VMEM((3, 128, 768), BF),
+            pltpu.VMEM((3, 128, D), BF),
+            pltpu.VMEM((3, 128, D), BF),
+            pltpu.VMEM((3, 128, D), BF),
+            pltpu.VMEM((8, 16, 128), F32),
+            pltpu.VMEM((7, 16, 128), F32),
+            pltpu.VMEM((4, 16, 128), F32),
+            pltpu.SemaphoreType.DMA((160,)),
+            pltpu.SemaphoreType.DMA((160,)),
+            pltpu.SemaphoreType.DMA((24,)),
+        ],
+        compiler_params=pltpu.CompilerParams(
+            collective_id=0, has_side_effects=True, vmem_limit_bytes=VMEM_LIMIT
+        ),
+        cost_estimate=pl.CostEstimate(flops=26_000_000_000, bytes_accessed=30_000_000, transcendentals=8_000_000),
+    )(xin, dmin, bias, pack, qkv_weight, out_weight, up_weight, down_weight)
+    out, d_input, gq, go, gu, gd, small = outs
+    grad_qkv = gq.reshape(4, 128, 3, 256).transpose(1, 2, 0, 3).reshape(128, 3072).astype(F32)
+    grad_up = gu.reshape(4, 128, 8, 128).transpose(1, 2, 0, 3).reshape(128, 4096).astype(F32)
+    grad_down = gd.reshape(512, D).astype(F32)
+    return (
+        out[:, :tok], d_input[:, :tok], small[0], small[1], grad_qkv, small[2], small[3],
+        go.astype(F32), small[4], small[5], small[6], grad_up, small[8:12].reshape(512), grad_down, small[7],
+    )
+
+
 def solution(mesh):
     in_specs = (
         P("shard", "seq", None),
@@ -422,6 +1117,7 @@
         P("shard", None),
         P("shard"),
     )
+    fits = dict(mesh.shape) == {"seq": NSEQ, "shard": NSH}
     return jax.shard_map(
-        per_device, mesh=mesh, in_specs=in_specs, out_specs=out_specs, check_vma=False
-    )
+        fused_device if fits else per_device, mesh=mesh, in_specs=in_specs, out_specs=out_specs, check_vma=False
+    )

time: 1060 us -> 260 us (0.25)
  waiting for transfers between devices: 619 us -> 0 us
  Pallas kernels: 0 us -> 235 us
  blocking collectives: 179 us -> 0 us
  matrix products: 117 us -> 0 us
  local copies, waits for them, and re-layouts: 63.6 us -> 15.9 us
  other arithmetic: 34.7 us -> 5.23 us
  starting transfers between devices: 20 us -> 0 us
  between operations: 16.2 us -> 0.88 us
    reduce_scatter x4 -> x0, waiting for transfers between devices: 369 us -> none  [the longest x1 153 us: reduce_grads(): lax.psum_scatter(grads[9].astype(jnp.bfloat16), 'shard', scatter_dimensio...]
    pallas_call x0 -> x1, Pallas kernels: none -> 235 us  [fused_device(): pl.pallas_call(layer_kernel, out_shape=(shape((2, TOK, D)), shape((2, TOK...]
    all_gather x4 -> x0, waiting for transfers between devices: 166 us -> none  [the longest x1 117 us: per_device(): lax.all_gather(shard_set[11], 'shard', axis=0, tiled=True)]
    all_gather x9 -> x0, blocking collectives: 139 us -> none  [the longest x1 22.9 us: per_device(): lax.all_gather(shard_set[10], 'shard', axis=0, tiled=True)]
    dot_general x18 -> x0, matrix products: 117 us -> none  [the longest x4 31.9 us: product_nt(): lax.dot_general(left, right, (((1,), (1,)), ((), ())), preferred_element_...]
    all_to_all x4 -> x0, waiting for transfers between devices: 65.5 us -> none  [the longest x1 36.1 us: layer_forward(): lax.all_to_all(packed, 'seq', split_axis=3, concat_axis=1, tiled=True)]
    unnamed x1 -> x0, blocking collectives: 28 us -> none
    reshape x10 -> x2, local copies, waits for them, and re-layouts: 26.6 us -> 1.34 us  [the longest x1 1.26 us: fused_device(): small[8:12].reshape(512)]
  transfers between devices with their start and end apart: 13 -> 0, of which waited for: 10 -> 0; matrix products, arithmetic and copies ran while one was open for 16% -> 0% of each run, Pallas kernels for 0% -> 0%
where the time goes in v1:
time: 260 us; the launch traced here: 257 us
  Pallas kernels  235 us (90%)
  local copies, waits for them, and re-layouts  15.9 us (6%)
  other arithmetic  5.23 us (2%)
    pallas_call x1, Pallas kernels, fused_device(): pl.pallas_call(layer_kernel, out_shape=(shape((2, TOK, D)), shape((2, TOK...  235 us
    unnamed x37, local copies, waits for them, and re-layouts  6.18 us

profile of v1, /device:TPU:1, one launch (start us, length us, event | category | flops | bytes accessed | tf_op | source)
XLA Modules:
  0.0 256.6 jit_solution(17665856182159520242)
XLA Ops:
  0.6 0.0 copy-start
  0.7 0.0 copy-start.8
  0.7 0.0 copy-start.9
  0.7 0.0 copy-start.10
  0.7 0.0 copy-start.11
  0.7 0.0 copy-start.12
  0.8 0.8 dynamic-slice_compare_fusion
  1.6 1.3 copy_select_fusion
  2.9 0.0 copy-start.7
  2.9 0.9 pad.18.dmin
  3.8 0.1 dynamic-slice_bitcast_fusion
  3.9 0.1 stack.39
  4.0 0.6 pad_convert_fusion.pack
  4.6 0.1 copy.43
  4.8 0.9 pad.17.xin
  5.7 0.1 reshape.68
  5.8 0.1 select_n.25
  5.9 1.1 broadcast_in_dim.30.bias
  6.9 234.5 %shard_map.271 = (bf16[2,160,1024]{2,1,0:T(8,128)(2,1)}, bf16[2,160,1024]{2,1,0:T(8,128)(2,1)}, bf16[4,128,768]{2,1,0:T(8,128)(2,1)}, bf16[128,1024]{1,0:T(8,128...) custom-call(bf16[2,160,1024]{2,1,0:T(8,128)(2,1)} %pad.17.xin, ...), custom_call_target="tpu_custom_call" | custom-call | flops 25999998976 | bytes 30000000 | tf_op jit(solution)/shard_map/pallas_call | solution.py:1018
  241.5 1.5 slice_bitcast_fusion.1
  243.0 1.3 slice_bitcast_fusion
  244.2 1.5 copy.51
  245.7 0.1 bitcast_bitcast_fusion
  245.9 1.4 copy.47
  247.2 1.9 reshape.71
  249.1 0.3 copy.45
  249.4 0.1 copy.46
  249.5 1.6 copy.50
  251.1 1.6 bitcast_convert_fusion
  252.8 1.4 copy.48
  254.3 1.4 copy.49
  255.7 0.8 convert_element_type.43
  (28 shorter events, 0.1 us)
Async XLA Ops:
  0.6 3.2 %copy-start = (bf16[512]{0:T(512)(128)(2,1)S(1)}, bf16[512]{0:T(512)(128)(2,1)}, u32[]{:S(2)}) copy-start(bf16[512]{0:T(512)(128)(2,1)} %param.29) | copy-start | bytes 3076
  0.7 3.2 %copy-start.8 = (bf16[128]{0:T(256)(128)(2,1)S(1)}, bf16[128]{0:T(256)(128)(2,1)}, u32[]{:S(2)}) copy-start(bf16[128]{0:T(256)(128)(2,1)} %param.19) | copy-start | bytes 772
  0.7 3.2 %copy-start.9 = (bf16[128]{0:T(256)(128)(2,1)S(1)}, bf16[128]{0:T(256)(128)(2,1)}, u32[]{:S(2)}) copy-start(bf16[128]{0:T(256)(128)(2,1)} %param.20) | copy-start | bytes 772
  0.7 3.2 %copy-start.10 = (bf16[128]{0:T(256)(128)(2,1)S(1)}, bf16[128]{0:T(256)(128)(2,1)}, u32[]{:S(2)}) copy-start(bf16[128]{0:T(256)(128)(2,1)} %param.22) | copy-start | bytes 772
  0.7 3.2 %copy-start.11 = (bf16[128]{0:T(256)(128)(2,1)S(1)}, bf16[128]{0:T(256)(128)(2,1)}, u32[]{:S(2)}) copy-start(bf16[128]{0:T(256)(128)(2,1)} %param.23) | copy-start | bytes 772
  0.7 3.2 %copy-start.12 = (bf16[128]{0:T(256)(128)(2,1)S(1)}, bf16[128]{0:T(256)(128)(2,1)}, u32[]{:S(2)}) copy-start(bf16[128]{0:T(256)(128)(2,1)} %param.25) | copy-start | bytes 772
  0.7 3.2 %copy-start.13 = (bf16[128]{0:T(256)(128)(2,1)S(1)}, bf16[128]{0:T(256)(128)(2,1)}, u32[]{:S(2)}) copy-start(bf16[128]{0:T(256)(128)(2,1)} %param.26) | copy-start | bytes 772
  0.7 3.2 %copy-start.14 = (bf16[128]{0:T(256)(128)(2,1)S(1)}, bf16[128]{0:T(256)(128)(2,1)}, u32[]{:S(2)}) copy-start(bf16[128]{0:T(256)(128)(2,1)} %param.27) | copy-start | bytes 772
  0.7 3.2 %copy-start.15 = (bf16[128]{0:T(256)(128)(2,1)S(1)}, bf16[128]{0:T(256)(128)(2,1)}, u32[]{:S(2)}) copy-start(bf16[128]{0:T(256)(128)(2,1)} %param.31) | copy-start | bytes 772
  0.7 3.9 %copy-start.3 = (bf16[2,146,1024]{2,0,1:T(2,128)(2,1)S(1)}, bf16[2,146,1024]{2,0,1:T(2,128)(2,1)}, u32[]{:S(2)}) copy-start(bf16[2,146,1024]{2,0,1:T(2,128)(2,1)} %param.16) | copy-start | bytes 1794052
  2.9 2.8 %copy-start.7 = (s32[2,584]{1,0:T(2,128)S(1)}, s32[2,584]{1,0:T(2,128)}, u32[]{:S(2)}) copy-start(s32[2,584]{1,0:T(2,128)} %param.17) | copy-start | bytes 14020
  247.2 1.9 copy-start.2
  249.5 1.6 copy-start.1
  251.1 1.6 copy-start.5
  251.1 3.1 %copy-start.4 = (bf16[2,160,1024]{2,1,0:T(8,128)(2,1)S(1)}, bf16[2,160,1024]{2,1,0:T(8,128)(2,1)}, u32[]{:S(2)}) copy-start(bf16[2,160,1024]{2,1,0:T(8,128)(2,1)} %get-tuple-element.23) | copy-start | bytes 1966084
  252.8 2.9 %copy-start.6 = (bf16[128,1024]{1,0:T(8,128)(2,1)S(1)}, bf16[128,1024]{1,0:T(8,128)(2,1)}, u32[]{:S(2)}) copy-start(bf16[128,1024]{1,0:T(8,128)(2,1)} %get-tuple-element.26) | copy-start | bytes 786436

commit v2 on v1

--- a/solution.py
+++ b/solution.py
@@ -388,6 +388,7 @@
     )
 
 
+LIMITS = (3, 4, 4, 6, 7, 8, 9, 10, 10, 10)
 NSEQ = 4
 NSH = 8
 TOK = 160
@@ -395,6 +396,7 @@
 HEADS_DEV = 4
 MASKED = -1e30
 VMEM_LIMIT = 64 * 1024 * 1024 - 1024 * 1024
+WIDEN_LIMIT = 32 * 1024 * 1024
 MESH_ID = pl.DeviceIdType.MESH
 BF = jnp.bfloat16
 F32 = jnp.float32
@@ -416,7 +418,7 @@
 def layer_kernel(
     xin, dmin, bias, pack, wq_h, wo_h, wu_h, wd_h,
     out_o, dx_o, gq_o, go_o, gu_o, gd_o, sg_o,
-    xg, wq, wo, wu, wd, pg, qkv, dqkv, probs, mixt, mixed, part, rc, rx, rc2, rx2,
+    bias_t, xg, wq, wo, wu, wd, pg, qkv, dqkv, probs, mixt, mixed, part, rc, rx, rc2, rx2,
     hid, cg, act, gate, dmg, dhid, dmix,
     gq, go, gu, gd, ryq, ryo, ryu, ryd, rzq, rzo, rzu, rzd, sgs, sg1, sg2,
     ssem, rsem, lsem,
@@ -471,10 +473,10 @@
     def rows(block):
         return pl.ds(pl.multiple_of(block * TOK, TOK), TOK)
 
-    def tiles(count, step, body, init=None):
+    def tiles(count, step, body, init=None, unroll=False):
         def inner(t, carry):
             return body(pl.multiple_of(t * step, step), carry)
-        return lax.fori_loop(0, count // step, inner, init)
+        return lax.fori_loop(0, count // step, inner, init, unroll=unroll)
 
     barrier = pltpu.get_barrier_semaphore()
     for d in range(1, NSEQ):
@@ -487,6 +489,11 @@
                     wu.at[j, :, pl.ds(128 * c, 128)]) for c in range(8)]
     load_d = load(("wd",), wd_h.at[pl.ds(pl.multiple_of(128 * s, 128), 128)], wd.at[j])
     pg[j] = pack[...]
+    n_wo = local.setdefault("wo", len(local))
+
+    @pl.when(z == s)
+    def _():
+        pltpu.make_async_copy(wo_h, wo.at[y], lsem.at[n_wo]).start()
     pl.semaphore_wait(barrier, NSEQ - 1 + NSH - 1)
 
     def ag4_start(key, buf, i, src):
@@ -501,18 +508,88 @@
         arrived((key, "c", i), buf.at[i, rows(s_core)], core)
         arrived((key, "d", i), buf.at[i, rows(s_diag)], core)
 
-    def agw_start(key, buf):
-        send(key, (key, "y", 0), buf.at[j], buf.at[j], ydev)
-        for d in (1, 2, 3):
-            send(key, (key, "z", d), buf.at[j], buf.at[j], (s, zj(d)))
-
-    def agw_forward(key, buf, d):
+    weights = {"wq": wq, "wu": wu, "wd": wd}
+    n_up, n_down = ix("wo", "up"), ix("wo", "down")
+
+    def out_hop(step):
+        n = n_up if step == 1 else n_down
+        return pltpu.make_async_remote_copy(
+            src_ref=wo.at[y], dst_ref=wo.at[y], send_sem=ssem.at[n], recv_sem=rsem.at[n_up],
+            device_id=(s, (z + step) * 2 + y), device_id_type=MESH_ID)
+
+    def out_hops(act_on):
+        @pl.when((z >= s) & (z < 3))
+        def _():
+            act_on(out_hop(1))
+
+        @pl.when((z <= s) & (z > 0))
+        def _():
+            act_on(out_hop(-1))
+
+    def gather_start(key, d):
+        if key == "wo":
+            @pl.when(z == s)
+            def _():
+                pltpu.make_async_copy(wo_h, wo.at[y], lsem.at[n_wo]).wait()
+
+            @pl.when((z == s) & (z < 3))
+            def _():
+                out_hop(1).start()
+
+            @pl.when((z == s) & (z > 0))
+            def _():
+                out_hop(-1).start()
+            return
+        buf = weights[key]
+        if d == 1:
+            send(key, (key, "y", 0), buf.at[j], buf.at[j], ydev)
+        send(key, (key, "z", d), buf.at[j], buf.at[j], (s, zj(d)))
+
+    def gather_forward(key, d):
+        if key == "wo":
+            @pl.when(z > s)
+            def _():
+                pltpu.make_async_remote_copy(
+                    src_ref=wo.at[y], dst_ref=wo.at[y], send_sem=ssem.at[n_up], recv_sem=rsem.at[n_up],
+                    device_id=(s, (z - 1) * 2 + y), device_id_type=MESH_ID).wait_recv()
+
+            @pl.when(z < s)
+            def _():
+                pltpu.make_async_remote_copy(
+                    src_ref=wo.at[y], dst_ref=wo.at[y], send_sem=ssem.at[n_up], recv_sem=rsem.at[n_up],
+                    device_id=(s, (z + 1) * 2 + y), device_id_type=MESH_ID).wait_recv()
+
+            @pl.when((z > s) & (z < 3))
+            def _():
+                out_hop(1).start()
+
+            @pl.when((z < s) & (z > 0))
+            def _():
+                out_hop(-1).start()
+            send("wo", ("wo", "y"), wo.at[y], wo.at[y], ydev)
+            return
+        buf = weights[key]
         jf = zj(4 - d)
         arrived((key, "z", d), buf.at[jf], (s, jf))
         send(key, (key, "y", d), buf.at[jf], buf.at[jf], ydev)
 
+    rounds = [("wq", 1), ("wq", 3), ("wq", 2), ("wo", 0), ("wu", 1), ("wu", 3), ("wu", 2), ("wd", 1), ("wd", 3), ("wd", 2)]
+    at_round, issued = [0], [0]
+
+    def gather_issue(upto):
+        while issued[0] < min(upto, len(rounds)):
+            gather_start(*rounds[issued[0]])
+            issued[0] += 1
+
+    def pump(count=1):
+        for _step in range(count):
+            n = at_round[0]
+            gather_forward(*rounds[n])
+            at_round[0] = n + 1
+            gather_issue(LIMITS[n])
+
     def agw_end(key, buf):
-        for d in (0, 1, 2, 3):
+        for d in (0, 1, 3, 2):
             jf = lax.rem(z + 4 - d, 4) * 2 + (1 - y)
             arrived((key, "y", d), buf.at[jf], ydev)
 
@@ -527,7 +604,7 @@
             here = pl.ds(pl.multiple_of(s_x * TOK + r, 32), 32)
             total = part[i, here, :].astype(F32) + rcb[i, 1, pl.ds(r, 32), :].astype(F32)
             part[i, here, :] = total.astype(BF)
-        tiles(TOK, 32, add)
+        tiles(TOK, 32, add, unroll=True)
         send(key, (key, "x", i), part.at[i, rows(s_x)], rxb.at[i], xdev)
 
     def rs4_wait(key, i, rcb, rxb):
@@ -545,21 +622,59 @@
             for ref, at in others:
                 total = total + ref[at, pl.ds(r, 32), :].astype(F32)
             g[row, pl.ds(r, 32), :] = total.astype(BF)
-        tiles(128, 32, add)
-
-    def rsw_start(key, g, ry):
-        for d in (1, 2, 3, 0):
-            send(key, (key, "gy", d), g.at[lax.rem(z + d, 4) * 2 + (1 - y)], ry.at[d], ydev)
-
-    def rsw_mid(key, g, ry, rz):
-        for d in (1, 2, 3, 0):
+        tiles(128, 32, add, unroll=True)
+
+    waiting, flying = [], []
+
+    def reduce_fill():
+        while waiting and len(flying) < 3:
+            piece = waiting.pop(0)
+            key, d, g, ry, rz = piece
+            if key == "o":
+                send("go", ("go", "y"), g.at[1 - y], ry, ydev)
+            else:
+                send(key, (key, "gy", d), g.at[lax.rem(z + d, 4) * 2 + (1 - y)], ry.at[d], ydev)
+            flying.append(piece)
+
+    def reduce_add(key, g, ry, rz):
+        for d in ((0,) if key == "o" else (2, 1, 3, 0)):
+            waiting.append((key, d, g, ry, rz))
+        reduce_fill()
+
+    def reduce_step(count=1):
+        for _step in range(count):
+            key, d, g, ry, rz = flying.pop(0)
+            if key == "o":
+                arrived(("go", "y"), ry, ydev)
+                reduce_fill()
+                add_out_block()
+                continue
             arrived((key, "gy", d), ry.at[d], ydev)
+            reduce_fill()
             add_into(g, zj(d), [(ry, d)])
             if d:
                 send(key, (key, "gz", d), g.at[zj(d)], rz.at[d - 1], (s, zj(d)))
 
+    n_gz = [ix("goz", d) for d in range(3)]
+    n_gs = ix("gozs")
+
+    def out_grad_copy(slot):
+        return pltpu.make_async_remote_copy(
+            src_ref=go.at[y], dst_ref=rzo.at[slot], send_sem=ssem.at[n_gs], recv_sem=rsem.at[n_gz[0] + slot],
+            device_id=(s, s * 2 + y), device_id_type=MESH_ID)
+
+    def add_out_block():
+        def add_out(r, _):
+            total = go[y, pl.ds(r, 32), :].astype(F32) + ryo[pl.ds(r, 32), :].astype(F32)
+            go[y, pl.ds(r, 32), :] = total.astype(BF)
+        tiles(128, 32, add_out, unroll=True)
+
+        @pl.when(z != s)
+        def _():
+            out_grad_copy(lax.rem(z + 3 - s, 4)).start()
+
     def rsw_end(key, g, rz, g_o):
-        for d in (1, 2, 3):
+        for d in (2, 1, 3):
             arrived((key, "gz", d), rz.at[d - 1], (s, zj(4 - d)))
         add_into(g, j, [(rz, 0), (rz, 1), (rz, 2)])
         copy = load((key, "go"), g.at[j], g_o.at[s])
@@ -595,20 +710,26 @@
     def fold(value):
         return value[0:8] + value[8:16] + value[16:24] + value[24:32]
 
-    for i in range(2):
-        ag4_start("xg", xg, i, xin.at[i])
     for d in range(1, NSH):
         send("pk", ("pk", d), pack, pg.at[j], (s, lax.rem(j + d, NSH)))
+    for i in range(2):
+        ag4_start("xg", xg, i, xin.at[i])
+    bias_t[...] = bias[...].T
     for copy in loads_q:
         copy.wait()
-    agw_start("wq", wq)
+    gather_issue(2)
     for i in range(2):
         xg[i, rows(s), :] = xin[i]
         dmg[i, rows(s), :] = dmin[i]
+    for copy in loads_u:
+        copy.wait()
+    load_d.wait()
+    pump()
+    ag4_forward("xg", xg, 0)
+
     for d in range(1, NSH):
         jf = lax.rem(j + NSH - d, NSH)
         arrived(("pk", d), pg.at[jf], (s, jf))
-
     attn_gain, attn_shift = param(0), param(1)
 
     def norm_block(i, block):
@@ -616,61 +737,38 @@
             here = pl.ds(pl.multiple_of(block * TOK + r, 32), 32)
             scaled, _inverse = normal(xg[i, here, :].astype(F32))
             xg[i, here, :] = (scaled * attn_gain + attn_shift).astype(BF)
-        tiles(TOK, 32, body)
+        tiles(TOK, 32, body, unroll=True)
 
     norm_block(0, s)
     norm_block(1, s)
-    ag4_forward("xg", xg, 0)
-    agw_forward("wq", wq, 1)
-    agw_forward("wq", wq, 2)
+    pump()
+    for i in range(2):
+        arrived(("xg", "c", i), xg.at[i, rows(s_core)], core)
+        norm_block(i, s_core)
     ag4_forward("xg", xg, 1)
-    agw_forward("wq", wq, 3)
-    for copy in loads_u:
-        copy.wait()
-    load_d.wait()
-
-    n_oz = [ix("woz", d) for d in (1, 2, 3)]
-
-    def out_copy(d):
-        return pltpu.make_async_remote_copy(
-            src_ref=wo.at[y], dst_ref=wo.at[y], send_sem=ssem.at[n_oz[d - 1]], recv_sem=rsem.at[n_oz[0]],
-            device_id=(s, zj(d)), device_id_type=MESH_ID)
-
-    @pl.when(z == s)
-    def _():
-        copy = pltpu.make_async_copy(wo_h, wo.at[y], lsem.at[local.setdefault("wo", len(local))])
-        copy.start()
-        copy.wait()
-        for d in (1, 2, 3):
-            out_copy(d).start()
-
-    agw_start("wu", wu)
-
-    for i in range(2):
-        ag4_end("xg", xg, i)
-        sent("xgf")
-        norm_block(i, s_core)
-        norm_block(i, s_x)
-        norm_block(i, s_diag)
     for i in range(2):
         ag4_start("dm", dmg, i, dmin.at[i])
+    arrived(("xg", "d", 0), xg.at[0, rows(s_diag)], core)
+    norm_block(0, s_diag)
+    sent("xgf")
+    pump()
+    norm_block(0, s_x)
+    norm_block(1, s_x)
+    arrived(("xg", "d", 1), xg.at[1, rows(s_diag)], core)
+    norm_block(1, s_diag)
+    pump()
     agw_end("wq", wq)
 
-    @pl.when(z != s)
-    def _():
-        pltpu.make_async_remote_copy(
-            src_ref=wo.at[y], dst_ref=wo.at[y], send_sem=ssem.at[n_oz[0]], recv_sem=rsem.at[n_oz[0]],
-            device_id=(s, zj(1)), device_id_type=MESH_ID).wait_recv()
-    send("wo", ("wo", "y"), wo.at[y], wo.at[y], ydev)
-
     packed_bias = jnp.concatenate([head_param(2), jnp.zeros((1, 256), F32), head_param(3)], axis=1)
 
-    def attend(i):
+    def project_in(i):
         def project(r, _):
             here = pl.ds(r, 320)
             value = dot_nn(xg[i, here, :], wq[...].reshape(D, 768)) + packed_bias
             qkv[i, here, :] = value.astype(BF)
         tiles(ROWS, 320, project)
+
+    def attend(i):
         value_t = qkv[i, :, 512:768].astype(F32).T.astype(BF)
         mixt[...] = value_t
         lane = lax.broadcasted_iota(jnp.int32, (1, 256), 1) // HEAD_DIM
@@ -678,7 +776,7 @@
         def one_head(h, _):
             keyed = jnp.where(lane == h, qkv[i, :, 256:512], jnp.zeros((), BF))
             query = qkv[i, :, 0:256] * jnp.asarray(HEAD_DIM ** -0.5, BF)
-            scores = dot_nt(keyed, query) + bias[i, :, 0:1]
+            scores = dot_nt(keyed, query) + bias_t[:, i:i + 1]
             raised = jnp.exp(scores - jnp.max(scores, axis=0, keepdims=True))
             chances = (raised * (1.0 / jnp.sum(raised, axis=0, keepdims=True))).astype(BF)
             probs[i, h] = chances
@@ -693,21 +791,21 @@
             part[i, here, :] = dot_nn(mixed[i, here, :], wo[...].reshape(256, D)).astype(BF)
         tiles(ROWS, 320, body)
 
+    project_in(0)
     attend(0)
-    agw_forward("wu", wu, 1)
+    project_in(1)
     arrived(("wo", "y"), wo.at[1 - y], ydev)
     project_out(0)
     rs4_a("o", 0, rc)
-    agw_forward("wu", wu, 2)
-    agw_forward("wu", wu, 3)
-    agw_start("wd", wd)
+    attend(1)
     rs4_b("o", 0, rc, rx)
-    attend(1)
     project_out(1)
     rs4_a("o", 1, rc)
+    pump()
     rs4_b("o", 1, rc, rx)
     for i in range(2):
         ag4_forward("dm", dmg, i)
+    pump()
 
     out_bias, mlp_gain, mlp_shift, down_bias = param(4), param(5), param(6), param(7)
     up_bias = param(8)
@@ -721,17 +819,14 @@
             scaled, _inverse = normal(value)
             here = pl.ds(pl.multiple_of(s * TOK + r, 32), 32)
             cg[i, here, :] = (scaled * mlp_gain + mlp_shift).astype(BF)
-        tiles(TOK, 32, middle)
+        tiles(TOK, 32, middle, unroll=True)
         ag4_start("c", cg, i, cg.at[i, rows(s)])
-    agw_forward("wd", wd, 1)
-    agw_forward("wd", wd, 2)
-    agw_forward("wd", wd, 3)
+        pump()
+    for n in range(2):
+        ag4_end("dm", dmg, n)
     agw_end("wu", wu)
     for i in range(2):
         ag4_forward("c", cg, i)
-        if i == 0:
-            for n in range(2):
-                ag4_end("dm", dmg, n)
         ag4_end("c", cg, i)
 
         def up(r, _, i=i):
@@ -741,18 +836,8 @@
             act[i, here, :] = (value * sig).astype(BF)
             gate[i, here, :] = (sig + GATE * value * sig * (1.0 - sig)).astype(BF)
         tiles(ROWS, 320, up)
-    agw_end("wd", wd)
+        pump()
     sent("o")
-
-    du_sum = jnp.zeros((8, D), F32)
-    for i in range(2):
-        def d_up(r, carry, i=i):
-            here = pl.ds(r, 320)
-            value = dot_nt(dmg[i, here, :], wd[...].reshape(D, D)) * gate[i, here, :].astype(F32)
-            value = value.astype(BF)
-            gate[i, here, :] = value
-            return carry + jnp.sum(value.astype(F32).reshape(40, 8, D), axis=0)
-        du_sum = tiles(ROWS, 320, d_up, du_sum)
 
     def weight_grad(left, right, g):
         def body(t, _):
@@ -761,23 +846,39 @@
             g[pl.ds(2 * t, 2)] = value.astype(BF).reshape(2, 128, right.shape[2])
         lax.fori_loop(0, left.shape[2] // 256, body, None)
 
-    sent("dmf")
-    sent("dm")
     weight_grad(act, dmg, gd)
-    rsw_start("d", gd, ryd)
+    reduce_add("d", gd, ryd, rzd)
+    agw_end("wd", wd)
+
+    def d_up(i, total):
+        def body(r, carry):
+            here = pl.ds(r, 320)
+            value = dot_nt(dmg[i, here, :], wd[...].reshape(D, D)) * gate[i, here, :].astype(F32)
+            value = value.astype(BF)
+            gate[i, here, :] = value
+            return carry + jnp.sum(value.astype(F32).reshape(40, 8, D), axis=0)
+        return tiles(ROWS, 320, body, total)
 
     def d_second(i):
         def body(r, _):
             here = pl.ds(r, 320)
             part[i, here, :] = dot_nt(gate[i, here, :], wu[...].reshape(D, D)).astype(BF)
         tiles(ROWS, 320, body)
-    for i in range(2):
-        d_second(i)
-        rs4_a("dc", i, rc)
+
+    sent("dmf")
+    sent("dm")
+    du_sum = d_up(0, jnp.zeros((8, D), F32))
+    d_second(0)
+    rs4_a("dc", 0, rc)
+    du_sum = d_up(1, du_sum)
     rs4_b("dc", 0, rc, rx)
+    d_second(1)
+    rs4_a("dc", 1, rc)
+    reduce_step()
     rs4_b("dc", 1, rc, rx)
     weight_grad(cg, gate, gu)
-    rsw_start("u", gu, ryu)
+    reduce_add("u", gu, ryu, rzu)
+    reduce_step()
 
     zero8 = jnp.zeros((8, D), F32)
     sums = (zero8, zero8, zero8, zero8)
@@ -795,8 +896,9 @@
             dmg[i, pl.ds(pl.multiple_of(s * TOK + r, 32), 32), :] = low
             return (carry[0] + fold(incoming * scaled), carry[1] + fold(incoming),
                     carry[2] + fold(low.astype(F32)), carry[3] + fold(upstream))
-        sums = tiles(TOK, 32, d_middle, sums)
+        sums = tiles(TOK, 32, d_middle, sums, unroll=True)
         ag4_start("db", dmg, i, dmg.at[i, rows(s)])
+        reduce_step()
     sent("dc")
 
     for i in range(2):
@@ -804,26 +906,12 @@
             here = pl.ds(r, 320)
             part[i, here, :] = dot_nn(act[i, here, :], wd[...].reshape(D, D)).astype(BF)
         tiles(ROWS, 320, down)
-    rsw_mid("d", gd, ryd, rzd)
-    for i in range(2):
-        ag4_forward("db", dmg, i)
-    for i in range(2):
-        ag4_end("db", dmg, i)
-    for i in range(2):
-        rs4_a("y", i, rc2)
-
-    for i in range(2):
-        def d_mixed(r, _, i=i):
+
+    def attend_back(i):
+        def d_mixed(r, _):
             here = pl.ds(r, 320)
             dmix[i, here, :] = dot_nt(dmg[i, here, :], wo[...].reshape(256, D)).astype(BF)
         tiles(ROWS, 320, d_mixed)
-    value = dot_tn(mixed[...].reshape(2 * ROWS, 256), dmg[...].reshape(2 * ROWS, D))
-    go[...] = value.astype(BF).reshape(2, 128, D)
-    send("go", ("go", "y"), go.at[1 - y], ryo, ydev)
-    rs4_b("y", 0, rc2, rx2)
-    rs4_b("y", 1, rc2, rx2)
-
-    def attend_back(i):
         lane = lax.broadcasted_iota(jnp.int32, (1, 256), 1) // HEAD_DIM
         mixt[...] = qkv[i, :, 256:512].astype(F32).T.astype(BF)
 
@@ -844,49 +932,54 @@
         lax.fori_loop(0, HEADS_DEV, one_head, None)
         dqkv[i, :, 0:256] = mixt[...].astype(F32).T.astype(BF)
 
-    attend_back(0)
-    rsw_mid("u", gu, ryu, rzu)
-    copy_d = rsw_end("d", gd, rzd, gd_o)
-    arrived(("go", "y"), ryo, ydev)
-
-    def add_out(r, _):
-        total = go[y, pl.ds(r, 32), :].astype(F32) + ryo[pl.ds(r, 32), :].astype(F32)
-        go[y, pl.ds(r, 32), :] = total.astype(BF)
-    tiles(128, 32, add_out)
-    n_gz = [ix("goz", d) for d in range(3)]
-    n_gs = ix("gozs")
-
-    def out_grad_copy(slot):
-        return pltpu.make_async_remote_copy(
-            src_ref=go.at[y], dst_ref=rzo.at[slot], send_sem=ssem.at[n_gs], recv_sem=rsem.at[n_gz[0] + slot],
-            device_id=(s, s * 2 + y), device_id_type=MESH_ID)
-
-    @pl.when(z != s)
-    def _():
-        out_grad_copy(lax.rem(z + 3 - s, 4)).start()
-
-    attend_back(1)
-    sent("y")
-    for i in range(2):
-        rs4_wait("y", i, rc2, rx2)
-
-        def last(r, _, i=i):
+    def out_presum(i):
+        arrived(("y", "c0", i), rc2.at[i, 0], core)
+        arrived(("y", "c1", i), rc2.at[i, 1], core)
+
+        def body(r, _):
             mine = pl.ds(r, 32)
-            value = hid[i, mine, :] + (rs4_sum(i, r, rc2, rx2) + down_bias)
-            out_o[i, mine, :] = value.astype(BF)
-        tiles(TOK, 32, last)
-    for i in range(2):
-        def d_normed(r, _, i=i):
+            here = pl.ds(pl.multiple_of(s * TOK + r, 32), 32)
+            there = pl.ds(pl.multiple_of(s_x * TOK + r, 32), 32)
+            total = part[i, here, :].astype(F32) + rc2[i, 0, mine, :].astype(F32)
+            hid[i, mine, :] = hid[i, mine, :] + (total + down_bias)
+            total = part[i, there, :].astype(F32) + rc2[i, 1, mine, :].astype(F32)
+            rc2[i, 1, mine, :] = total.astype(BF)
+        tiles(TOK, 32, body, unroll=True)
+
+    def d_normed(i):
+        def body(r, _):
             here = pl.ds(r, 320)
             part[i, here, :] = dot_nt(dqkv[i, here, :], wq[...].reshape(D, 768)).astype(BF)
-        tiles(ROWS, 320, d_normed)
+        tiles(ROWS, 320, body)
         rs4_a("da", i, rc)
+
+    ag4_forward("db", dmg, 0)
+    ag4_end("db", dmg, 0)
+    for i in range(2):
+        rs4_a("y", i, rc2)
+    attend_back(0)
+    reduce_step()
+    ag4_forward("db", dmg, 1)
+    for i in range(2):
+        out_presum(i)
+    sent("y")
+    d_normed(0)
+    ag4_end("db", dmg, 1)
+    copy_d = rsw_end("d", gd, rzd, gd_o)
     rs4_b("da", 0, rc, rx)
+    attend_back(1)
+    reduce_step()
+    d_normed(1)
+    weight_grad(xg, dqkv, gq)
     rs4_b("da", 1, rc, rx)
-    weight_grad(xg, dqkv, gq)
-    rsw_start("q", gq, ryq)
-
-    copy_u = rsw_end("u", gu, rzu, gu_o)
+    value = dot_tn(mixed[...].reshape(2 * ROWS, 256), dmg[...].reshape(2 * ROWS, D))
+    go[...] = value.astype(BF).reshape(2, 128, D)
+    reduce_add("o", go, ryo, rzo)
+    reduce_add("q", gq, ryq, rzq)
+    reduce_step()
+    for i in range(2):
+        send("y", ("y", "x", i), rc2.at[i, 1], rx2.at[i], xdev)
+    reduce_step()
 
     n_gb = [ix("gob", d) for d in range(3)]
 
@@ -895,24 +988,6 @@
             src_ref=go.at[y], dst_ref=go_o, send_sem=ssem.at[n_gb[d - 1]], recv_sem=rsem.at[n_gb[0]],
             device_id=(lax.rem(s + d, 4), j), device_id_type=MESH_ID)
     n_ol = local.setdefault("go", len(local))
-
-    @pl.when(z == s)
-    def _():
-        for slot in range(3):
-            pltpu.make_async_remote_copy(
-                src_ref=go.at[y], dst_ref=rzo.at[slot], send_sem=ssem.at[n_gs], recv_sem=rsem.at[n_gz[slot]],
-                device_id=(s, zj(1)), device_id_type=MESH_ID).wait_recv()
-
-        def add(r, _):
-            total = go[y, pl.ds(r, 32), :].astype(F32)
-            for slot in range(3):
-                total = total + rzo[slot, pl.ds(r, 32), :].astype(F32)
-            go[y, pl.ds(r, 32), :] = total.astype(BF)
-        tiles(128, 32, add)
-        pltpu.make_async_copy(go.at[y], go_o, lsem.at[n_ol]).start()
-        for d in (1, 2, 3):
-            out_final_copy(d).start()
-    rsw_forward("d", gd_o)
 
     sums_a = (zero8, zero8)
     for i in range(2):
@@ -925,7 +1000,10 @@
             value = dhid[i, mine, :] + normal_back(incoming, scaled, inverse, attn_gain)
             dx_o[i, mine, :] = value.astype(BF)
             return carry[0] + fold(incoming * scaled), carry[1] + fold(incoming)
-        sums_a = tiles(TOK, 32, d_input, sums_a)
+        sums_a = tiles(TOK, 32, d_input, sums_a, unroll=True)
+        if i == 0:
+            rsw_forward("d", gd_o)
+            reduce_step()
 
     sgs[...] = jnp.zeros_like(sgs)
 
@@ -954,7 +1032,25 @@
     for d in range(1, NSH):
         send("sg", ("sg", d), sgs.at[lax.rem(j + d, NSH)], sg1.at[d - 1], (s, lax.rem(j + d, NSH)))
 
-    rsw_mid("q", gq, ryq, rzq)
+    copy_u = rsw_end("u", gu, rzu, gu_o)
+    reduce_step(2)
+
+    @pl.when(z == s)
+    def _():
+        for slot in range(3):
+            pltpu.make_async_remote_copy(
+                src_ref=go.at[y], dst_ref=rzo.at[slot], send_sem=ssem.at[n_gs], recv_sem=rsem.at[n_gz[slot]],
+                device_id=(s, zj(1)), device_id_type=MESH_ID).wait_recv()
+
+        def add(r, _):
+            total = go[y, pl.ds(r, 32), :].astype(F32)
+            for slot in range(3):
+                total = total + rzo[slot, pl.ds(r, 32), :].astype(F32)
+            go[y, pl.ds(r, 32), :] = total.astype(BF)
+        tiles(128, 32, add, unroll=True)
+        pltpu.make_async_copy(go.at[y], go_o, lsem.at[n_ol]).start()
+        for d in (1, 2, 3):
+            out_final_copy(d).start()
 
     for d in range(1, NSH):
         jf = lax.rem(j + NSH - d, NSH)
@@ -965,6 +1061,15 @@
     sg2[0] = total
     for d in range(1, NSEQ):
         send("sg", ("sh", d), sg2.at[0], sg2.at[d], (lax.rem(s + d, NSEQ), j))
+    for i in range(2):
+        arrived(("y", "x", i), rx2.at[i], xdev)
+
+        def last(r, _, i=i):
+            mine = pl.ds(r, 32)
+            out_o[i, mine, :] = (hid[i, mine, :] + rx2[i, mine, :].astype(F32)).astype(BF)
+        tiles(TOK, 32, last, unroll=True)
+    reduce_step(len(flying) + len(waiting))
+    assert not waiting and not flying
     rsw_forward("u", gu_o)
     copy_q = rsw_end("q", gq, rzq, gq_o)
     for d in range(1, NSEQ):
@@ -979,7 +1084,6 @@
     def _():
         for d in (1, 2, 3):
             out_final_copy(d).wait_send()
-            out_copy(d).wait_send()
         pltpu.make_async_copy(go.at[y], go_o, lsem.at[n_ol]).wait()
 
     @pl.when(z != s)
@@ -988,8 +1092,25 @@
         out_grad_copy(0).wait_send()
     for copy in (copy_d, copy_u, copy_q):
         copy.wait()
+    out_hops(lambda hop: hop.wait_send())
     for tag in list(pending):
         sent(tag)
+
+def widen_kernel(
+    gq, go, gu, gd, small,
+    attn_gain, attn_shift, qkv, query, value, out, out_b, mlp_gain, mlp_shift, up, up_b, down, down_b,
+):
+    for at, ref in enumerate((attn_gain, attn_shift, query, value, out_b, mlp_gain, mlp_shift, down_b)):
+        ref[...] = small[at]
+    for b in range(NSEQ):
+        up_b[128 * b:128 * b + 128] = small[8 + b]
+        for c in range(3):
+            qkv[:, 1024 * c + 256 * b:1024 * c + 256 * b + 256] = gq[b, :, 256 * c:256 * c + 256].astype(F32)
+        for c in range(8):
+            up[:, 512 * c + 128 * b:512 * c + 128 * b + 128] = gu[b, :, 128 * c:128 * c + 128].astype(F32)
+        down[128 * b:128 * b + 128, :] = gd[b].astype(F32)
+    out[...] = go[...].astype(F32)
+
 
 def fused_device(
     inputs, key_mask, cotangent, attn_gain, attn_shift, qkv_weight, query_bias, value_bias,
@@ -997,13 +1118,15 @@
 ):
     tok = inputs.shape[1]
     s = lax.axis_index("seq")
-    own_mask = lax.dynamic_slice_in_dim(key_mask, s * tok, tok, 1)
-    gap = ((0, 0), (0, TOK - tok), (0, 0))
-    xin = jnp.pad(inputs, gap)
-    dmin = jnp.pad(jnp.where(own_mask[:, :, None] > 0, cotangent, jnp.zeros((), BF)), gap)
-    slots = jnp.pad(key_mask.reshape(2, NSEQ, tok), ((0, 0), (0, 0), (0, TOK - tok)))
-    bias = jnp.where(slots.reshape(2, ROWS, 1) > 0, 0.0, MASKED)
-    bias = jnp.broadcast_to(bias, (2, ROWS, 128)).astype(F32)
+    gap = ((0, 0), (0, TOK - tok))
+    slots = jnp.pad(key_mask.reshape(2, NSEQ, tok), ((0, 0),) + gap)
+    own_mask = lax.dynamic_slice_in_dim(slots, s, 1, 1).reshape(2, TOK, 1)
+    held = lax.broadcasted_iota(jnp.int32, (1, TOK, 1), 1) < tok
+    none = jnp.zeros((), BF)
+    xin = jnp.where(held, jnp.pad(inputs, gap + ((0, 0),)), none)
+    dmin = jnp.where(own_mask > 0, jnp.pad(cotangent, gap + ((0, 0),)), none)
+    bias = jnp.where(slots.reshape(2, ROWS) > 0, 0.0, MASKED).astype(F32)
+    bias = jnp.pad(bias, ((0, 6), (0, 0)))
     own_up = lax.dynamic_slice_in_dim(up_bias, s * 128, 128, 0)
     pack = jnp.stack(
         (attn_gain, attn_shift, query_bias, value_bias, out_bias, mlp_gain, mlp_shift, down_bias, own_up)
@@ -1024,6 +1147,7 @@
         in_specs=[vm, vm, vm, vm, hbm, hbm, hbm, hbm],
         out_specs=(vm, vm, hbm, hbm, hbm, hbm, vm),
         scratch_shapes=[
+            pltpu.VMEM((ROWS, 8), F32),
             pltpu.VMEM((2, ROWS, D), BF),
             pltpu.VMEM((8, 128, 768), BF),
             pltpu.VMEM((2, 128, D), BF),
@@ -1072,13 +1196,18 @@
         cost_estimate=pl.CostEstimate(flops=26_000_000_000, bytes_accessed=30_000_000, transcendentals=8_000_000),
     )(xin, dmin, bias, pack, qkv_weight, out_weight, up_weight, down_weight)
     out, d_input, gq, go, gu, gd, small = outs
-    grad_qkv = gq.reshape(4, 128, 3, 256).transpose(1, 2, 0, 3).reshape(128, 3072).astype(F32)
-    grad_up = gu.reshape(4, 128, 8, 128).transpose(1, 2, 0, 3).reshape(128, 4096).astype(F32)
-    grad_down = gd.reshape(512, D).astype(F32)
-    return (
-        out[:, :tok], d_input[:, :tok], small[0], small[1], grad_qkv, small[2], small[3],
-        go.astype(F32), small[4], small[5], small[6], grad_up, small[8:12].reshape(512), grad_down, small[7],
-    )
+    line = shape((128,), F32)
+    grads = pl.pallas_call(
+        widen_kernel,
+        out_shape=(
+            line, line, shape((128, 3 * D), F32), line, line, shape((128, D), F32), line, line, line,
+            shape((128, 4 * D), F32), shape((512,), F32), shape((512, D), F32), line,
+        ),
+        in_specs=[vm] * 5,
+        out_specs=(vm,) * 13,
+        compiler_params=pltpu.CompilerParams(vmem_limit_bytes=WIDEN_LIMIT),
+    )(gq, go, gu, gd, small)
+    return (out[:, :tok], d_input[:, :tok]) + tuple(grads)
 
 
 def solution(mesh):

time: 260 us -> 213 us (0.82)
  Pallas kernels: 235 us -> 197 us
  local copies, waits for them, and re-layouts: 15.9 us -> 9.58 us
  other arithmetic: 5.23 us -> 1.97 us
    pallas_call x1, Pallas kernels: 235 us -> 193 us  [fused_device(): pl.pallas_call(layer_kernel, out_shape=(shape((2, TOK, D)), shape((2, TOK...]
    convert_element_type x5 -> x0, local copies, waits for them, and re-layouts: 3.72 us -> none  [the longest x3 3.34 us: fused_device(): gu.reshape(4, 128, 8, 128).transpose(1, 2, 0, 3).reshape(128, 4096)]
    pallas_call x0 -> x1, Pallas kernels: none -> 3.15 us  [fused_device(): pl.pallas_call(widen_kernel, out_shape=(line, line, shape((128, 3 * D), F...]
    unnamed x37 -> x18, local copies, waits for them, and re-layouts: 6.18 us -> 5.98 us
where the time goes in v2:
time: 213 us; the launch traced here: 209 us
  Pallas kernels  197 us (92%)
  local copies, waits for them, and re-layouts  9.58 us (4%)
    pallas_call x1, Pallas kernels, fused_device(): pl.pallas_call(layer_kernel, out_shape=(shape((2, TOK, D)), shape((2, TOK...  193 us
    unnamed x18, local copies, waits for them, and re-layouts  5.98 us

profile of v2, /device:TPU:1, one launch (start us, length us, event | category | flops | bytes accessed | tf_op | source)
XLA Modules:
  0.0 209.1 jit_solution(15902174989263686137)
XLA Ops:
  0.6 0.0 copy-start
  0.7 0.7 copy-done
  1.3 0.1 dynamic-slice_bitcast_fusion
  1.4 0.8 stack.39
  2.2 0.6 pad_convert_fusion.pack
  2.8 0.8 reshape.54
  3.7 0.1 select_n.25
  3.7 0.6 pad.24.bias
  4.4 1.2 copy.35
  5.6 1.2 copy.37
  6.8 1.3 pad_select_fusion
  8.1 193.4 %shard_map.271 = (bf16[2,160,1024]{2,1,0:T(8,128)(2,1)}, bf16[2,160,1024]{2,1,0:T(8,128)(2,1)}, bf16[4,128,768]{2,1,0:T(8,128)(2,1)}, bf16[128,1024]{1,0:T(8,128...) custom-call(bf16[2,160,1024]{2,1,0:T(8,128)(2,1)} %get-tuple-element.86.xin, ...), custom_call_target="tpu_custom_call" | custom-call | flops 25999998976 | bytes 30000000 | tf_op jit(solution)/shard_map/pallas_call | solution.py:1141
  201.6 0.0 copy-start.6
  201.6 1.2 slice.6
  202.8 0.0 copy-start.1
  202.8 0.0 copy-start.2
  202.8 0.0 copy-start.3
  202.8 0.0 copy-start.4
  202.8 0.0 copy-start.5
  202.8 1.4 copy.39
  204.3 0.0 copy-done.6
  204.3 1.4 copy.40
  205.8 0.0 copy-done.1
  205.8 0.0 copy-done.2
  205.8 0.0 copy-done.3
  205.8 0.0 copy-done.4
  205.8 0.0 copy-done.5
  205.8 3.1 %shard_map.272 = (f32[128]{0:T(128)}, f32[128]{0:T(128)}, f32[128,3072]{1,0:T(8,128)}, f32[128]{0:T(128)}, f32[128]{0:T(128)}, /*index=5*/f32[128,1024]{1,0:T(8,...) custom-call(bf16[4,128,768]{2,1,0:T(8,128)(2,1)S(1)} %copy-done.3, ...), custom_call_target="tpu_custom_call" | custom-call | tf_op jit(solution)/shard_map/pallas_call | solution.py:1200
  (6 shorter events, 0.1 us)
Async XLA Ops:
  0.6 0.7 copy-start
  201.6 2.7 %copy-start.6 = (bf16[2,160,1024]{2,1,0:T(8,128)(2,1)S(1)}, bf16[2,160,1024]{2,1,0:T(8,128)(2,1)}, u32[]{:S(2)}) copy-start(bf16[2,160,1024]{2,1,0:T(8,128)(2,1)} %get-tuple-element.36) | copy-start | bytes 1966084
  202.8 3.0 %copy-start.1 = (bf16[4,128,1024]{2,1,0:T(8,128)(2,1)S(1)}, bf16[4,128,1024]{2,1,0:T(8,128)(2,1)}, u32[]{:S(2)}) copy-start(bf16[4,128,1024]{2,1,0:T(8,128)(2,1)} %get-tuple-element.39.gu) | copy-start | bytes 3145732
  202.8 3.0 %copy-start.2 = (bf16[4,128,1024]{2,1,0:T(8,128)(2,1)S(1)}, bf16[4,128,1024]{2,1,0:T(8,128)(2,1)}, u32[]{:S(2)}) copy-start(bf16[4,128,1024]{2,1,0:T(8,128)(2,1)} %get-tuple-element.40.gd) | copy-start | bytes 3145732
  202.8 3.0 %copy-start.3 = (bf16[4,128,768]{2,1,0:T(8,128)(2,1)S(1)}, bf16[4,128,768]{2,1,0:T(8,128)(2,1)}, u32[]{:S(2)}) copy-start(bf16[4,128,768]{2,1,0:T(8,128)(2,1)} %get-tuple-element.37.gq) | copy-start | bytes 2359300
  202.8 2.9 %copy-start.4 = (bf16[128,1024]{1,0:T(8,128)(2,1)S(1)}, bf16[128,1024]{1,0:T(8,128)(2,1)}, u32[]{:S(2)}) copy-start(bf16[128,1024]{1,0:T(8,128)(2,1)} %get-tuple-element.38.go) | copy-start | bytes 786436
  202.8 2.9 %copy-start.5 = (f32[16,128]{1,0:T(8,128)S(1)}, f32[16,128]{1,0:T(8,128)}, u32[]{:S(2)}) copy-start(f32[16,128]{1,0:T(8,128)} %get-tuple-element.41.small) | copy-start | bytes 24580

commit v3 on v2

--- a/solution.py
+++ b/solution.py
@@ -388,7 +388,11 @@
     )
 
 
-LIMITS = (3, 4, 4, 6, 7, 8, 9, 10, 10, 10)
+STEPS = (1, 3, 2)
+PUMPS = (1, 1, 1, 0, 0, 0, 0, 1, 1, 1, 1, 1, 1, 0, 1)
+LIMITS = (2, 3, 3, 4, 6, 7, 8, 9, 10, 10, 10)
+MT = 640
+FLIGHT = 99
 NSEQ = 4
 NSH = 8
 TOK = 160
@@ -396,7 +400,7 @@
 HEADS_DEV = 4
 MASKED = -1e30
 VMEM_LIMIT = 64 * 1024 * 1024 - 1024 * 1024
-WIDEN_LIMIT = 32 * 1024 * 1024
+WIDEN_LIMIT = 64 * 1024 * 1024 - 1024 * 1024
 MESH_ID = pl.DeviceIdType.MESH
 BF = jnp.bfloat16
 F32 = jnp.float32
@@ -416,9 +420,9 @@
 
 
 def layer_kernel(
-    xin, dmin, bias, pack, wq_h, wo_h, wu_h, wd_h,
+    inp, cot, kmask, b0, b1, b2, b3, b4, b5, b6, b7, b8, wq_h, wo_h, wu_h, wd_h,
     out_o, dx_o, gq_o, go_o, gu_o, gd_o, sg_o,
-    bias_t, xg, wq, wo, wu, wd, pg, qkv, dqkv, probs, mixt, mixed, part, rc, rx, rc2, rx2,
+    xin, dmin, pack, bias_t, xg, wq, wo, wu, wd, pg, qkv, dqkv, probs, mixt, mixed, part, rc, rx, rc2, rx2,
     hid, cg, act, gate, dmg, dhid, dmix,
     gq, go, gu, gd, ryq, ryo, ryu, ryd, rzq, rzo, rzu, rzd, sgs, sg1, sg2,
     ssem, rsem, lsem,
@@ -427,6 +431,7 @@
     j = lax.axis_index("shard")
     x, k = s // 2, s % 2
     z, y = j // 2, j % 2
+    zs = k * 2 + x
     s_core = x * 2 + (1 - k)
     s_x = (1 - x) * 2 + k
     s_diag = (1 - x) * 2 + (1 - k)
@@ -483,15 +488,30 @@
         pl.semaphore_signal(barrier, inc=1, device_id=(lax.rem(s + d, NSEQ), j), device_id_type=MESH_ID)
     for d in range(1, NSH):
         pl.semaphore_signal(barrier, inc=1, device_id=(s, lax.rem(j + d, NSH)), device_id_type=MESH_ID)
-    loads_q = [load(("wq", c), wq_h.at[:, pl.ds(pl.multiple_of(1024 * c + 256 * s, 256), 256)],
+    loads_q = [load(("wq", c), wq_h.at[:, pl.ds(pl.multiple_of(1024 * c + 256 * zs, 256), 256)],
                     wq.at[j, :, pl.ds(256 * c, 256)]) for c in range(3)]
     loads_u = [load(("wu", c), wu_h.at[:, pl.ds(pl.multiple_of(512 * c + 128 * s, 128), 128)],
                     wu.at[j, :, pl.ds(128 * c, 128)]) for c in range(8)]
     load_d = load(("wd",), wd_h.at[pl.ds(pl.multiple_of(128 * s, 128), 128)], wd.at[j])
+    for row, ref in enumerate((b0, b1, b2, b3, b4, b5, b6, b7)):
+        pack[row:row + 1, :] = ref[...].astype(F32)
+    own_row = lax.broadcasted_iota(jnp.int32, (NSEQ, 128), 0) == s
+    pack[8:9, :] = jnp.sum(jnp.where(own_row, b8[...].astype(F32), 0.0), axis=0, keepdims=True)
+    pack[9:16, :] = jnp.zeros((7, 128), F32)
     pg[j] = pack[...]
+
+    tok = inp.shape[0]
+
+    def slots_of(source, i):
+        row = lax.broadcasted_iota(jnp.int32, (TOK, 2 * tok), 0)
+        col = lax.broadcasted_iota(jnp.int32, (TOK, 2 * tok), 1)
+        chosen = (col == 2 * row + i).astype(F32).astype(BF)
+        return dot_nn(chosen, source[...].reshape(2 * tok, D))
+    for i in range(2):
+        xin[i] = slots_of(inp, i).astype(BF)
     n_wo = local.setdefault("wo", len(local))
 
-    @pl.when(z == s)
+    @pl.when(z == zs)
     def _():
         pltpu.make_async_copy(wo_h, wo.at[y], lsem.at[n_wo]).start()
     pl.semaphore_wait(barrier, NSEQ - 1 + NSH - 1)
@@ -509,89 +529,75 @@
         arrived((key, "d", i), buf.at[i, rows(s_diag)], core)
 
     weights = {"wq": wq, "wu": wu, "wd": wd}
-    n_up, n_down = ix("wo", "up"), ix("wo", "down")
-
-    def out_hop(step):
-        n = n_up if step == 1 else n_down
+    n_oz, n_oy = [ix("wo", d) for d in (1, 2, 3)], ix("wo", "y")
+
+    def out_copy(d):
         return pltpu.make_async_remote_copy(
-            src_ref=wo.at[y], dst_ref=wo.at[y], send_sem=ssem.at[n], recv_sem=rsem.at[n_up],
-            device_id=(s, (z + step) * 2 + y), device_id_type=MESH_ID)
-
-    def out_hops(act_on):
-        @pl.when((z >= s) & (z < 3))
+            src_ref=wo.at[y], dst_ref=wo.at[y], send_sem=ssem.at[n_oz[d - 1]], recv_sem=rsem.at[n_oz[0]],
+            device_id=(s, zj(d)), device_id_type=MESH_ID)
+
+    def out_start():
+        @pl.when(z == zs)
         def _():
-            act_on(out_hop(1))
-
-        @pl.when((z <= s) & (z > 0))
+            pltpu.make_async_copy(wo_h, wo.at[y], lsem.at[n_wo]).wait()
+            for d in (2, 1, 3):
+                out_copy(d).start()
+
+    def out_forward():
+        @pl.when(z != zs)
         def _():
-            act_on(out_hop(-1))
+            pltpu.make_async_remote_copy(
+                src_ref=wo.at[y], dst_ref=wo.at[y], send_sem=ssem.at[n_oz[0]], recv_sem=rsem.at[n_oz[0]],
+                device_id=(s, zs * 2 + y), device_id_type=MESH_ID).wait_recv()
+        send("wo", ("wo", "y"), wo.at[y], wo.at[y], ydev)
+
+    def block_rows(d):
+        return (2, pl.ds(64 * (d - 20), 64)) if d >= 20 else (d, pl.ds(0, 128))
 
     def gather_start(key, d):
         if key == "wo":
-            @pl.when(z == s)
-            def _():
-                pltpu.make_async_copy(wo_h, wo.at[y], lsem.at[n_wo]).wait()
-
-            @pl.when((z == s) & (z < 3))
-            def _():
-                out_hop(1).start()
-
-            @pl.when((z == s) & (z > 0))
-            def _():
-                out_hop(-1).start()
+            out_start()
             return
         buf = weights[key]
         if d == 1:
             send(key, (key, "y", 0), buf.at[j], buf.at[j], ydev)
-        send(key, (key, "z", d), buf.at[j], buf.at[j], (s, zj(d)))
+        step, part_rows = block_rows(d)
+        mine = buf.at[j, part_rows]
+        send(key, (key, "z", d), mine, mine, (s, zj(step)))
 
     def gather_forward(key, d):
         if key == "wo":
-            @pl.when(z > s)
-            def _():
-                pltpu.make_async_remote_copy(
-                    src_ref=wo.at[y], dst_ref=wo.at[y], send_sem=ssem.at[n_up], recv_sem=rsem.at[n_up],
-                    device_id=(s, (z - 1) * 2 + y), device_id_type=MESH_ID).wait_recv()
-
-            @pl.when(z < s)
-            def _():
-                pltpu.make_async_remote_copy(
-                    src_ref=wo.at[y], dst_ref=wo.at[y], send_sem=ssem.at[n_up], recv_sem=rsem.at[n_up],
-                    device_id=(s, (z + 1) * 2 + y), device_id_type=MESH_ID).wait_recv()
-
-            @pl.when((z > s) & (z < 3))
-            def _():
-                out_hop(1).start()
-
-            @pl.when((z < s) & (z > 0))
-            def _():
-                out_hop(-1).start()
-            send("wo", ("wo", "y"), wo.at[y], wo.at[y], ydev)
+            out_forward()
             return
         buf = weights[key]
-        jf = zj(4 - d)
-        arrived((key, "z", d), buf.at[jf], (s, jf))
-        send(key, (key, "y", d), buf.at[jf], buf.at[jf], ydev)
-
-    rounds = [("wq", 1), ("wq", 3), ("wq", 2), ("wo", 0), ("wu", 1), ("wu", 3), ("wu", 2), ("wd", 1), ("wd", 3), ("wd", 2)]
+        step, part_rows = block_rows(d)
+        jf = zj(4 - step)
+        block = buf.at[jf, part_rows]
+        arrived((key, "z", d), block, (s, jf))
+        send(key, (key, "y", d), block, block, ydev)
+
+    issue_order = [("wq", d) for d in STEPS] + [("wo", 0)]
+    issue_order += [(key, d) for key in ("wu", "wd") for d in STEPS]
+    rounds = list(issue_order)
     at_round, issued = [0], [0]
 
     def gather_issue(upto):
         while issued[0] < min(upto, len(rounds)):
-            gather_start(*rounds[issued[0]])
+            gather_start(*issue_order[issued[0]])
             issued[0] += 1
 
-    def pump(count=1):
-        for _step in range(count):
+    def pump(place):
+        for _step in range(PUMPS[place]):
             n = at_round[0]
             gather_forward(*rounds[n])
             at_round[0] = n + 1
-            gather_issue(LIMITS[n])
+            gather_issue(LIMITS[n + 1])
 
     def agw_end(key, buf):
-        for d in (0, 1, 3, 2):
-            jf = lax.rem(z + 4 - d, 4) * 2 + (1 - y)
-            arrived((key, "y", d), buf.at[jf], ydev)
+        for d in (0,) + STEPS:
+            step, part_rows = block_rows(d)
+            jf = lax.rem(z + 4 - step, 4) * 2 + (1 - y)
+            arrived((key, "y", d), buf.at[jf, part_rows], ydev)
 
     def rs4_a(key, i, rcb):
         send(key, (key, "c0", i), part.at[i, rows(s_core)], rcb.at[i, 0], core)
@@ -627,7 +633,7 @@
     waiting, flying = [], []
 
     def reduce_fill():
-        while waiting and len(flying) < 3:
+        while waiting and len(flying) < FLIGHT:
             piece = waiting.pop(0)
             key, d, g, ry, rz = piece
             if key == "o":
@@ -661,7 +667,7 @@
     def out_grad_copy(slot):
         return pltpu.make_async_remote_copy(
             src_ref=go.at[y], dst_ref=rzo.at[slot], send_sem=ssem.at[n_gs], recv_sem=rsem.at[n_gz[0] + slot],
-            device_id=(s, s * 2 + y), device_id_type=MESH_ID)
+            device_id=(s, zs * 2 + y), device_id_type=MESH_ID)
 
     def add_out_block():
         def add_out(r, _):
@@ -669,9 +675,9 @@
             go[y, pl.ds(r, 32), :] = total.astype(BF)
         tiles(128, 32, add_out, unroll=True)
 
-        @pl.when(z != s)
+        @pl.when(z != zs)
         def _():
-            out_grad_copy(lax.rem(z + 3 - s, 4)).start()
+            out_grad_copy(lax.rem(z + 3 - zs, 4)).start()
 
     def rsw_end(key, g, rz, g_o):
         for d in (2, 1, 3):
@@ -694,7 +700,7 @@
         return jnp.concatenate([pg[b, pl.ds(p, 1), :] for b in range(NSH)], axis=1)
 
     def head_param(p):
-        return jnp.concatenate([pg[2 * s, pl.ds(p, 1), :], pg[2 * s + 1, pl.ds(p, 1), :]], axis=1)
+        return jnp.concatenate([pg[2 * zs, pl.ds(p, 1), :], pg[2 * zs + 1, pl.ds(p, 1), :]], axis=1)
 
     def normal(value):
         centre = jnp.mean(value, axis=-1, keepdims=True)
@@ -714,17 +720,25 @@
         send("pk", ("pk", d), pack, pg.at[j], (s, lax.rem(j + d, NSH)))
     for i in range(2):
         ag4_start("xg", xg, i, xin.at[i])
-    bias_t[...] = bias[...].T
     for copy in loads_q:
         copy.wait()
-    gather_issue(2)
-    for i in range(2):
+    gather_issue(LIMITS[0])
+    slot = lax.broadcasted_iota(jnp.int32, (ROWS, 1), 0)
+    shift = sum(jnp.where(slot >= TOK * b, TOK - tok, 0) for b in range(1, NSEQ))
+    used = slot - sum(jnp.where(slot >= TOK * b, TOK, 0) for b in range(1, NSEQ)) < tok
+    place_of = jnp.where(used, slot - shift, -1)
+    chosen = lax.broadcasted_iota(jnp.int32, (ROWS, kmask.shape[1]), 1) == place_of
+    live = dot_nt(chosen.astype(F32).astype(BF), kmask[...].astype(F32).astype(BF))
+    bias_t[:, 0:2] = jnp.where(live > 0.5, 0.0, MASKED)
+    for i in range(2):
+        mask = bias_t[pl.ds(pl.multiple_of(s * TOK, TOK), TOK), i:i + 1]
+        dmin[i] = jnp.where(mask == 0.0, slots_of(cot, i), 0.0).astype(BF)
         xg[i, rows(s), :] = xin[i]
         dmg[i, rows(s), :] = dmin[i]
     for copy in loads_u:
         copy.wait()
     load_d.wait()
-    pump()
+    pump(0)
     ag4_forward("xg", xg, 0)
 
     for d in range(1, NSH):
@@ -741,7 +755,7 @@
 
     norm_block(0, s)
     norm_block(1, s)
-    pump()
+    pump(1)
     for i in range(2):
         arrived(("xg", "c", i), xg.at[i, rows(s_core)], core)
         norm_block(i, s_core)
@@ -751,26 +765,26 @@
     arrived(("xg", "d", 0), xg.at[0, rows(s_diag)], core)
     norm_block(0, s_diag)
     sent("xgf")
-    pump()
+    pump(2)
     norm_block(0, s_x)
     norm_block(1, s_x)
     arrived(("xg", "d", 1), xg.at[1, rows(s_diag)], core)
     norm_block(1, s_diag)
-    pump()
+    pump(3)
     agw_end("wq", wq)
 
     packed_bias = jnp.concatenate([head_param(2), jnp.zeros((1, 256), F32), head_param(3)], axis=1)
 
     def project_in(i):
         def project(r, _):
-            here = pl.ds(r, 320)
+            here = pl.ds(r, MT)
             value = dot_nn(xg[i, here, :], wq[...].reshape(D, 768)) + packed_bias
             qkv[i, here, :] = value.astype(BF)
-        tiles(ROWS, 320, project)
-
-    def attend(i):
-        value_t = qkv[i, :, 512:768].astype(F32).T.astype(BF)
-        mixt[...] = value_t
+        tiles(ROWS, MT, project)
+
+    def attend(i, first, last):
+        if first == 0:
+            mixt[...] = qkv[i, :, 512:768].astype(F32).T.astype(BF)
         lane = lax.broadcasted_iota(jnp.int32, (1, 256), 1) // HEAD_DIM
 
         def one_head(h, _):
@@ -782,30 +796,37 @@
             probs[i, h] = chances
             here = pl.ds(pl.multiple_of(h * HEAD_DIM, HEAD_DIM), HEAD_DIM)
             mixt[here, :] = dot_nn(mixt[here, :], chances).astype(BF)
-        lax.fori_loop(0, HEADS_DEV, one_head, None)
-        mixed[i] = mixt[...].astype(F32).T.astype(BF)
+        lax.fori_loop(first, last, one_head, None)
+        if last == HEADS_DEV:
+            mixed[i] = mixt[...].astype(F32).T.astype(BF)
 
     def project_out(i):
         def body(r, _):
-            here = pl.ds(r, 320)
+            here = pl.ds(r, MT)
             part[i, here, :] = dot_nn(mixed[i, here, :], wo[...].reshape(256, D)).astype(BF)
-        tiles(ROWS, 320, body)
+        tiles(ROWS, MT, body)
 
     project_in(0)
-    attend(0)
+    attend(0, 0, 2)
+    pump(14)
+    attend(0, 2, 4)
+    pump(4)
     project_in(1)
     arrived(("wo", "y"), wo.at[1 - y], ydev)
     project_out(0)
     rs4_a("o", 0, rc)
-    attend(1)
+    pump(5)
+    attend(1, 0, 2)
+    pump(6)
+    attend(1, 2, 4)
     rs4_b("o", 0, rc, rx)
     project_out(1)
     rs4_a("o", 1, rc)
-    pump()
+    pump(7)
     rs4_b("o", 1, rc, rx)
     for i in range(2):
         ag4_forward("dm", dmg, i)
-    pump()
+    pump(8)
 
     out_bias, mlp_gain, mlp_shift, down_bias = param(4), param(5), param(6), param(7)
     up_bias = param(8)
@@ -821,7 +842,7 @@
             cg[i, here, :] = (scaled * mlp_gain + mlp_shift).astype(BF)
         tiles(TOK, 32, middle, unroll=True)
         ag4_start("c", cg, i, cg.at[i, rows(s)])
-        pump()
+        pump(9 + i)
     for n in range(2):
         ag4_end("dm", dmg, n)
     agw_end("wu", wu)
@@ -830,40 +851,41 @@
         ag4_end("c", cg, i)
 
         def up(r, _, i=i):
-            here = pl.ds(r, 320)
+            here = pl.ds(r, MT)
             value = dot_nn(cg[i, here, :], wu[...].reshape(D, D)) + up_bias
             sig = jax.nn.sigmoid(GATE * value)
             act[i, here, :] = (value * sig).astype(BF)
             gate[i, here, :] = (sig + GATE * value * sig * (1.0 - sig)).astype(BF)
-        tiles(ROWS, 320, up)
-        pump()
+        tiles(ROWS, MT, up)
+        pump(11 + i)
     sent("o")
 
     def weight_grad(left, right, g):
         def body(t, _):
-            cols = pl.ds(pl.multiple_of(t * 256, 256), 256)
-            value = dot_tn(left[:, :, cols].reshape(2 * ROWS, 256), right[...].reshape(2 * ROWS, right.shape[2]))
-            g[pl.ds(2 * t, 2)] = value.astype(BF).reshape(2, 128, right.shape[2])
-        lax.fori_loop(0, left.shape[2] // 256, body, None)
+            cols = pl.ds(pl.multiple_of(t * 512, 512), 512)
+            value = dot_tn(left[:, :, cols].reshape(2 * ROWS, 512), right[...].reshape(2 * ROWS, right.shape[2]))
+            g[pl.ds(4 * t, 4)] = value.astype(BF).reshape(4, 128, right.shape[2])
+        lax.fori_loop(0, left.shape[2] // 512, body, None)
 
     weight_grad(act, dmg, gd)
+    pump(13)
     reduce_add("d", gd, ryd, rzd)
     agw_end("wd", wd)
 
     def d_up(i, total):
         def body(r, carry):
-            here = pl.ds(r, 320)
+            here = pl.ds(r, MT)
             value = dot_nt(dmg[i, here, :], wd[...].reshape(D, D)) * gate[i, here, :].astype(F32)
             value = value.astype(BF)
             gate[i, here, :] = value
-            return carry + jnp.sum(value.astype(F32).reshape(40, 8, D), axis=0)
-        return tiles(ROWS, 320, body, total)
+            return carry + jnp.sum(value.astype(F32).reshape(MT // 8, 8, D), axis=0)
+        return tiles(ROWS, MT, body, total)
 
     def d_second(i):
         def body(r, _):
-            here = pl.ds(r, 320)
+            here = pl.ds(r, MT)
             part[i, here, :] = dot_nt(gate[i, here, :], wu[...].reshape(D, D)).astype(BF)
-        tiles(ROWS, 320, body)
+        tiles(ROWS, MT, body)
 
     sent("dmf")
     sent("dm")
@@ -903,15 +925,15 @@
 
     for i in range(2):
         def down(r, _, i=i):
-            here = pl.ds(r, 320)
+            here = pl.ds(r, MT)
             part[i, here, :] = dot_nn(act[i, here, :], wd[...].reshape(D, D)).astype(BF)
-        tiles(ROWS, 320, down)
+        tiles(ROWS, MT, down)
 
     def attend_back(i):
         def d_mixed(r, _):
-            here = pl.ds(r, 320)
+            here = pl.ds(r, MT)
             dmix[i, here, :] = dot_nt(dmg[i, here, :], wo[...].reshape(256, D)).astype(BF)
-        tiles(ROWS, 320, d_mixed)
+        tiles(ROWS, MT, d_mixed)
         lane = lax.broadcasted_iota(jnp.int32, (1, 256), 1) // HEAD_DIM
         mixt[...] = qkv[i, :, 256:512].astype(F32).T.astype(BF)
 
@@ -948,9 +970,9 @@
 
     def d_normed(i):
         def body(r, _):
-            here = pl.ds(r, 320)
+            here = pl.ds(r, MT)
             part[i, here, :] = dot_nt(dqkv[i, here, :], wq[...].reshape(D, 768)).astype(BF)
-        tiles(ROWS, 320, body)
+        tiles(ROWS, MT, body)
         rs4_a("da", i, rc)
 
     ag4_forward("db", dmg, 0)
@@ -1022,8 +1044,8 @@
     d_query_sum = jnp.sum(dqkv[0, :, 0:256].astype(F32) + dqkv[1, :, 0:256].astype(F32), axis=0, keepdims=True)
     d_value_sum = jnp.sum(dqkv[0, :, 512:768].astype(F32) + dqkv[1, :, 512:768].astype(F32), axis=0, keepdims=True)
     for b in range(2):
-        sgs[2 * s + b, pl.ds(2, 1), :] = d_query_sum[:, 128 * b:128 * b + 128]
-        sgs[2 * s + b, pl.ds(3, 1), :] = d_value_sum[:, 128 * b:128 * b + 128]
+        sgs[2 * zs + b, pl.ds(2, 1), :] = d_query_sum[:, 128 * b:128 * b + 128]
+        sgs[2 * zs + b, pl.ds(3, 1), :] = d_value_sum[:, 128 * b:128 * b + 128]
     up_sum = flat(du_sum)
     row_at = lax.broadcasted_iota(jnp.int32, (8, 128), 0)
     for b in range(NSH):
@@ -1035,7 +1057,7 @@
     copy_u = rsw_end("u", gu, rzu, gu_o)
     reduce_step(2)
 
-    @pl.when(z == s)
+    @pl.when(z == zs)
     def _():
         for slot in range(3):
             pltpu.make_async_remote_copy(
@@ -1080,32 +1102,40 @@
     rsw_done("u", gu_o)
     rsw_done("q", gq_o)
 
-    @pl.when(z == s)
+    @pl.when(z == zs)
     def _():
         for d in (1, 2, 3):
             out_final_copy(d).wait_send()
         pltpu.make_async_copy(go.at[y], go_o, lsem.at[n_ol]).wait()
 
-    @pl.when(z != s)
+    @pl.when(z != zs)
     def _():
         out_final_copy(1).wait_recv()
         out_grad_copy(0).wait_send()
     for copy in (copy_d, copy_u, copy_q):
         copy.wait()
-    out_hops(lambda hop: hop.wait_send())
+
+    @pl.when(z == zs)
+    def _():
+        for d in (1, 2, 3):
+            out_copy(d).wait_send()
     for tag in list(pending):
         sent(tag)
 
 def widen_kernel(
-    gq, go, gu, gd, small,
-    attn_gain, attn_shift, qkv, query, value, out, out_b, mlp_gain, mlp_shift, up, up_b, down, down_b,
+    result, d_input, gq, go, gu, gd, small,
+    output, input_grad, attn_gain, attn_shift, qkv, query, value, out, out_b, mlp_gain, mlp_shift, up, up_b, down, down_b,
 ):
+    tok = output.shape[0]
+    for i in range(2):
+        output[:, i, :] = result[i, 0:tok, :]
+        input_grad[:, i, :] = d_input[i, 0:tok, :]
     for at, ref in enumerate((attn_gain, attn_shift, query, value, out_b, mlp_gain, mlp_shift, down_b)):
         ref[...] = small[at]
     for b in range(NSEQ):
         up_b[128 * b:128 * b + 128] = small[8 + b]
         for c in range(3):
-            qkv[:, 1024 * c + 256 * b:1024 * c + 256 * b + 256] = gq[b, :, 256 * c:256 * c + 256].astype(F32)
+            qkv[:, 1024 * c + 256 * b:1024 * c + 256 * b + 256] = gq[(b % 2) * 2 + b // 2, :, 256 * c:256 * c + 256].astype(F32)
         for c in range(8):
             up[:, 512 * c + 128 * b:512 * c + 128 * b + 128] = gu[b, :, 128 * c:128 * c + 128].astype(F32)
         down[128 * b:128 * b + 128, :] = gd[b].astype(F32)
@@ -1117,21 +1147,10 @@
     out_weight, out_bias, mlp_gain, mlp_shift, up_weight, up_bias, down_weight, down_bias,
 ):
     tok = inputs.shape[1]
-    s = lax.axis_index("seq")
-    gap = ((0, 0), (0, TOK - tok))
-    slots = jnp.pad(key_mask.reshape(2, NSEQ, tok), ((0, 0),) + gap)
-    own_mask = lax.dynamic_slice_in_dim(slots, s, 1, 1).reshape(2, TOK, 1)
-    held = lax.broadcasted_iota(jnp.int32, (1, TOK, 1), 1) < tok
-    none = jnp.zeros((), BF)
-    xin = jnp.where(held, jnp.pad(inputs, gap + ((0, 0),)), none)
-    dmin = jnp.where(own_mask > 0, jnp.pad(cotangent, gap + ((0, 0),)), none)
-    bias = jnp.where(slots.reshape(2, ROWS) > 0, 0.0, MASKED).astype(F32)
-    bias = jnp.pad(bias, ((0, 6), (0, 0)))
-    own_up = lax.dynamic_slice_in_dim(up_bias, s * 128, 128, 0)
-    pack = jnp.stack(
-        (attn_gain, attn_shift, query_bias, value_bias, out_bias, mlp_gain, mlp_shift, down_bias, own_up)
-    ).astype(F32)
-    pack = jnp.pad(pack, ((0, 7), (0, 0)))
+    lines = [
+        entry.reshape(1, 128)
+        for entry in (attn_gain, attn_shift, query_bias, value_bias, out_bias, mlp_gain, mlp_shift, down_bias)
+    ]
     vm = pl.BlockSpec(memory_space=pltpu.VMEM)
     hbm = pl.BlockSpec(memory_space=pl.ANY)
 
@@ -1144,9 +1163,12 @@
             shape((2, TOK, D)), shape((2, TOK, D)), shape((4, 128, 768)), shape((128, D)),
             shape((4, 128, D)), shape((4, 128, D)), shape((16, 128), F32),
         ),
-        in_specs=[vm, vm, vm, vm, hbm, hbm, hbm, hbm],
+        in_specs=[vm] * 12 + [hbm] * 4,
         out_specs=(vm, vm, hbm, hbm, hbm, hbm, vm),
         scratch_shapes=[
+            pltpu.VMEM((2, TOK, D), BF),
+            pltpu.VMEM((2, TOK, D), BF),
+            pltpu.VMEM((16, 128), F32),
             pltpu.VMEM((ROWS, 8), F32),
             pltpu.VMEM((2, ROWS, D), BF),
             pltpu.VMEM((8, 128, 768), BF),
@@ -1194,20 +1216,20 @@
             collective_id=0, has_side_effects=True, vmem_limit_bytes=VMEM_LIMIT
         ),
         cost_estimate=pl.CostEstimate(flops=26_000_000_000, bytes_accessed=30_000_000, transcendentals=8_000_000),
-    )(xin, dmin, bias, pack, qkv_weight, out_weight, up_weight, down_weight)
+    )(inputs.transpose(1, 0, 2), cotangent.transpose(1, 0, 2), key_mask, *lines, up_bias.reshape(NSEQ, 128), qkv_weight, out_weight, up_weight, down_weight)
     out, d_input, gq, go, gu, gd, small = outs
     line = shape((128,), F32)
     grads = pl.pallas_call(
         widen_kernel,
         out_shape=(
-            line, line, shape((128, 3 * D), F32), line, line, shape((128, D), F32), line, line, line,
+            shape((tok, 2, D)), shape((tok, 2, D)), line, line, shape((128, 3 * D), F32), line, line, shape((128, D), F32), line, line, line,
             shape((128, 4 * D), F32), shape((512,), F32), shape((512, D), F32), line,
         ),
-        in_specs=[vm] * 5,
-        out_specs=(vm,) * 13,
+        in_specs=[vm] * 7,
+        out_specs=(vm,) * 15,
         compiler_params=pltpu.CompilerParams(vmem_limit_bytes=WIDEN_LIMIT),
-    )(gq, go, gu, gd, small)
-    return (out[:, :tok], d_input[:, :tok]) + tuple(grads)
+    )(out, d_input, gq, go, gu, gd, small)
+    return (grads[0].transpose(1, 0, 2), grads[1].transpose(1, 0, 2)) + tuple(grads[2:])
 
 
 def solution(mesh):

time: 213 us -> 201 us (0.944)
  the two profiles are of different devices: /device:TPU:1 before, /device:TPU:9 now
where the time goes in v3:
time: 201 us; the launch traced here: 197 us
  Pallas kernels  196 us (98%)
    pallas_call x1, Pallas kernels, fused_device(): pl.pallas_call(layer_kernel, out_shape=(shape((2, TOK, D)), shape((2, TOK...  190 us
    pallas_call x1, Pallas kernels, fused_device(): pl.pallas_call(widen_kernel, out_shape=(shape((tok, 2, D)), shape((tok, 2...  5.65 us

profile of v3, /device:TPU:9, one launch (start us, length us, event | category | flops | bytes accessed | tf_op | source)
XLA Modules:
  0.0 196.9 jit_solution(2011282896537407277)
XLA Ops:
  0.7 190.1 %shard_map.271 = (bf16[2,160,1024]{2,1,0:T(8,128)(2,1)}, bf16[2,160,1024]{2,1,0:T(8,128)(2,1)}, bf16[4,128,768]{2,1,0:T(8,128)(2,1)}, bf16[128,1024]{1,0:T(8,128...) custom-call(bf16[146,2,1024]{2,1,0:T(2,128)(2,1)} %bitcast.13, ...), custom_call_target="tpu_custom_call" | custom-call | flops 25999998976 | bytes 30000000 | tf_op jit(solution)/shard_map/pallas_call | solution.py:1160
  190.8 5.6 %shard_map.272 = (bf16[146,2,1024]{2,1,0:T(2,128)(2,1)}, bf16[146,2,1024]{2,1,0:T(2,128)(2,1)}, f32[128]{0:T(128)}, f32[128]{0:T(128)}, f32[128,3072]{1,0:T(8,12...) custom-call(bf16[2,160,1024]{2,1,0:T(8,128)(2,1)} %get-tuple-element, ...), custom_call_target="tpu_custom_call" | custom-call | tf_op jit(solution)/shard_map/pallas_call | solution.py:1222

commit v4 on v3

--- a/solution.py
+++ b/solution.py
@@ -392,7 +392,7 @@
 PUMPS = (1, 1, 1, 0, 0, 0, 0, 1, 1, 1, 1, 1, 1, 0, 1)
 LIMITS = (2, 3, 3, 4, 6, 7, 8, 9, 10, 10, 10)
 MT = 640
-FLIGHT = 99
+FLIGHT = 3
 NSEQ = 4
 NSH = 8
 TOK = 160
@@ -449,6 +449,7 @@
         return ids.setdefault(key, len(ids))
 
     pending = {}
+    parts = part
 
     def send(tag, key, src, dst, dev):
         n = ix(*key)
@@ -600,11 +601,13 @@
             arrived((key, "y", d), buf.at[jf, part_rows], ydev)
 
     def rs4_a(key, i, rcb):
+        part = act if key == "da" else parts
         send(key, (key, "c0", i), part.at[i, rows(s_core)], rcb.at[i, 0], core)
         send(key, (key, "c1", i), part.at[i, rows(s_diag)], rcb.at[i, 1], core)
 
     def rs4_b(key, i, rcb, rxb):
         arrived((key, "c1", i), rcb.at[i, 1], core)
+        part = act if key == "da" else parts
 
         def add(r, _):
             here = pl.ds(pl.multiple_of(s_x * TOK + r, 32), 32)
@@ -617,7 +620,8 @@
         arrived((key, "c0", i), rcb.at[i, 0], core)
         arrived((key, "x", i), rxb.at[i], xdev)
 
-    def rs4_sum(i, r, rcb, rxb):
+    def rs4_sum(i, r, rcb, rxb, part=None):
+        part = parts if part is None else part
         here = pl.ds(pl.multiple_of(s * TOK + r, 32), 32)
         return (part[i, here, :].astype(F32) + rcb[i, 0, pl.ds(r, 32), :].astype(F32)
                 + rxb[i, pl.ds(r, 32), :].astype(F32))
@@ -971,7 +975,7 @@
     def d_normed(i):
         def body(r, _):
             here = pl.ds(r, MT)
-            part[i, here, :] = dot_nt(dqkv[i, here, :], wq[...].reshape(D, 768)).astype(BF)
+            act[i, here, :] = dot_nt(dqkv[i, here, :], wq[...].reshape(D, 768)).astype(BF)
         tiles(ROWS, MT, body)
         rs4_a("da", i, rc)
 
@@ -982,9 +986,6 @@
     attend_back(0)
     reduce_step()
     ag4_forward("db", dmg, 1)
-    for i in range(2):
-        out_presum(i)
-    sent("y")
     d_normed(0)
     ag4_end("db", dmg, 1)
     copy_d = rsw_end("d", gd, rzd, gd_o)
@@ -1000,6 +1001,7 @@
     reduce_add("q", gq, ryq, rzq)
     reduce_step()
     for i in range(2):
+        out_presum(i)
         send("y", ("y", "x", i), rc2.at[i, 1], rx2.at[i], xdev)
     reduce_step()
 
@@ -1011,22 +1013,6 @@
             device_id=(lax.rem(s + d, 4), j), device_id_type=MESH_ID)
     n_ol = local.setdefault("go", len(local))
 
-    sums_a = (zero8, zero8)
-    for i in range(2):
-        rs4_wait("da", i, rc, rx)
-
-        def d_input(r, carry, i=i):
-            mine = pl.ds(r, 32)
-            incoming = rs4_sum(i, r, rc, rx)
-            scaled, inverse = normal(xin[i, mine, :].astype(F32))
-            value = dhid[i, mine, :] + normal_back(incoming, scaled, inverse, attn_gain)
-            dx_o[i, mine, :] = value.astype(BF)
-            return carry[0] + fold(incoming * scaled), carry[1] + fold(incoming)
-        sums_a = tiles(TOK, 32, d_input, sums_a, unroll=True)
-        if i == 0:
-            rsw_forward("d", gd_o)
-            reduce_step()
-
     sgs[...] = jnp.zeros_like(sgs)
 
     def place(row, total):
@@ -1035,8 +1021,6 @@
 
     def flat(value):
         return jnp.sum(value, axis=0, keepdims=True)
-    place(0, flat(sums_a[0]))
-    place(1, flat(sums_a[1]))
     place(4, flat(sums[2]))
     place(5, flat(sums[0]))
     place(6, flat(sums[1]))
@@ -1051,6 +1035,24 @@
     for b in range(NSH):
         wide = jnp.broadcast_to(up_sum[:, 128 * b:128 * b + 128], (8, 128))
         sgs[b, 8:16, :] = jnp.where(row_at == s, wide, 0.0)
+    sums_a = (zero8, zero8)
+    for i in range(2):
+        rs4_wait("da", i, rc, rx)
+
+        def d_input(r, carry, i=i):
+            mine = pl.ds(r, 32)
+            incoming = rs4_sum(i, r, rc, rx, act)
+            scaled, inverse = normal(xin[i, mine, :].astype(F32))
+            value = dhid[i, mine, :] + normal_back(incoming, scaled, inverse, attn_gain)
+            dx_o[i, mine, :] = value.astype(BF)
+            return carry[0] + fold(incoming * scaled), carry[1] + fold(incoming)
+        sums_a = tiles(TOK, 32, d_input, sums_a, unroll=True)
+        if i == 0:
+            rsw_forward("d", gd_o)
+            reduce_step()
+
+    place(0, flat(sums_a[0]))
+    place(1, flat(sums_a[1]))
     for d in range(1, NSH):
         send("sg", ("sg", d), sgs.at[lax.rem(j + d, NSH)], sg1.at[d - 1], (s, lax.rem(j + d, NSH)))
 

time: 201 us -> 200 us (level)
  the two profiles are of different devices: /device:TPU:9 before, /device:TPU:1 now
where the time goes in v4:
time: 200 us; the launch traced here: 196 us
  Pallas kernels  195 us (98%)
    pallas_call x1, Pallas kernels, fused_device(): pl.pallas_call(layer_kernel, out_shape=(shape((2, TOK, D)), shape((2, TOK...  190 us
    pallas_call x1, Pallas kernels, fused_device(): pl.pallas_call(widen_kernel, out_shape=(shape((tok, 2, D)), shape((tok, 2...  5.65 us

profile of v4, /device:TPU:1, one launch (start us, length us, event | category | flops | bytes accessed | tf_op | source)
XLA Modules:
  0.0 196.3 jit_solution(4139786789875603644)
XLA Ops:
  0.7 189.5 %shard_map.271 = (bf16[2,160,1024]{2,1,0:T(8,128)(2,1)}, bf16[2,160,1024]{2,1,0:T(8,128)(2,1)}, bf16[4,128,768]{2,1,0:T(8,128)(2,1)}, bf16[128,1024]{1,0:T(8,128...) custom-call(bf16[146,2,1024]{2,1,0:T(2,128)(2,1)} %bitcast.13, ...), custom_call_target="tpu_custom_call" | custom-call | flops 25999998976 | bytes 30000000 | tf_op jit(solution)/shard_map/pallas_call | solution.py:1162
  190.2 5.6 %shard_map.272 = (bf16[146,2,1024]{2,1,0:T(2,128)(2,1)}, bf16[146,2,1024]{2,1,0:T(2,128)(2,1)}, f32[128]{0:T(128)}, f32[128]{0:T(128)}, f32[128,3072]{1,0:T(8,12...) custom-call(bf16[2,160,1024]{2,1,0:T(8,128)(2,1)} %get-tuple-element, ...), custom_call_target="tpu_custom_call" | custom-call | tf_op jit(solution)/shard_map/pallas_call | solution.py:1224

commit v5 on v4

--- a/solution.py
+++ b/solution.py
@@ -933,13 +933,14 @@
             part[i, here, :] = dot_nn(act[i, here, :], wd[...].reshape(D, D)).astype(BF)
         tiles(ROWS, MT, down)
 
-    def attend_back(i):
-        def d_mixed(r, _):
-            here = pl.ds(r, MT)
-            dmix[i, here, :] = dot_nt(dmg[i, here, :], wo[...].reshape(256, D)).astype(BF)
-        tiles(ROWS, MT, d_mixed)
+    def attend_back(i, first, last):
+        if first == 0:
+            def d_mixed(r, _):
+                here = pl.ds(r, MT)
+                dmix[i, here, :] = dot_nt(dmg[i, here, :], wo[...].reshape(256, D)).astype(BF)
+            tiles(ROWS, MT, d_mixed)
+            mixt[...] = qkv[i, :, 256:512].astype(F32).T.astype(BF)
         lane = lax.broadcasted_iota(jnp.int32, (1, 256), 1) // HEAD_DIM
-        mixt[...] = qkv[i, :, 256:512].astype(F32).T.astype(BF)
 
         def one_head(h, _):
             own = lane == h
@@ -955,8 +956,9 @@
             dqkv[i, :, 256:512] = jnp.where(own, d_key.astype(BF), dqkv[i, :, 256:512])
             here = pl.ds(pl.multiple_of(h * HEAD_DIM, HEAD_DIM), HEAD_DIM)
             mixt[here, :] = (dot_nn(mixt[here, :], d_scores) * HEAD_DIM ** -0.5).astype(BF)
-        lax.fori_loop(0, HEADS_DEV, one_head, None)
-        dqkv[i, :, 0:256] = mixt[...].astype(F32).T.astype(BF)
+        lax.fori_loop(first, last, one_head, None)
+        if last == HEADS_DEV:
+            dqkv[i, :, 0:256] = mixt[...].astype(F32).T.astype(BF)
 
     def out_presum(i):
         arrived(("y", "c0", i), rc2.at[i, 0], core)
@@ -983,14 +985,15 @@
     ag4_end("db", dmg, 0)
     for i in range(2):
         rs4_a("y", i, rc2)
-    attend_back(0)
+    attend_back(0, 0, 4)
     reduce_step()
     ag4_forward("db", dmg, 1)
     d_normed(0)
     ag4_end("db", dmg, 1)
     copy_d = rsw_end("d", gd, rzd, gd_o)
+    attend_back(1, 0, 2)
     rs4_b("da", 0, rc, rx)
-    attend_back(1)
+    attend_back(1, 2, 4)
     reduce_step()
     d_normed(1)
     weight_grad(xg, dqkv, gq)

time: 200 us -> 200 us (level)
  no operation moved by 1% of the time
where the time goes in v5:
time: 200 us; the launch traced here: 196 us
  Pallas kernels  195 us (98%)
    pallas_call x1, Pallas kernels, fused_device(): pl.pallas_call(layer_kernel, out_shape=(shape((2, TOK, D)), shape((2, TOK...  189 us
    pallas_call x1, Pallas kernels, fused_device(): pl.pallas_call(widen_kernel, out_shape=(shape((tok, 2, D)), shape((tok, 2...  5.65 us

profile of v5, /device:TPU:1, one launch (start us, length us, event | category | flops | bytes accessed | tf_op | source)
XLA Modules:
  0.0 195.9 jit_solution(5083670674734350032)
XLA Ops:
  0.7 189.1 %shard_map.271 = (bf16[2,160,1024]{2,1,0:T(8,128)(2,1)}, bf16[2,160,1024]{2,1,0:T(8,128)(2,1)}, bf16[4,128,768]{2,1,0:T(8,128)(2,1)}, bf16[128,1024]{1,0:T(8,128...) custom-call(bf16[146,2,1024]{2,1,0:T(2,128)(2,1)} %bitcast.13, ...), custom_call_target="tpu_custom_call" | custom-call | flops 25999998976 | bytes 30000000 | tf_op jit(solution)/shard_map/pallas_call | solution.py:1165
  189.8 5.6 %shard_map.272 = (bf16[146,2,1024]{2,1,0:T(2,128)(2,1)}, bf16[146,2,1024]{2,1,0:T(2,128)(2,1)}, f32[128]{0:T(128)}, f32[128]{0:T(128)}, f32[128,3072]{1,0:T(8,12...) custom-call(bf16[2,160,1024]{2,1,0:T(8,128)(2,1)} %get-tuple-element, ...), custom_call_target="tpu_custom_call" | custom-call | tf_op jit(solution)/shard_map/pallas_call | solution.py:1227

commit v6 on v5

--- a/solution.py
+++ b/solution.py
@@ -392,7 +392,7 @@
 PUMPS = (1, 1, 1, 0, 0, 0, 0, 1, 1, 1, 1, 1, 1, 0, 1)
 LIMITS = (2, 3, 3, 4, 6, 7, 8, 9, 10, 10, 10)
 MT = 640
-FLIGHT = 3
+FLIGHT = 5
 NSEQ = 4
 NSH = 8
 TOK = 160

time: 200 us -> 200 us (level)
  no operation moved by 1% of the time
where the time goes in v6:
time: 200 us; the launch traced here: 196 us
  Pallas kernels  195 us (98%)
    pallas_call x1, Pallas kernels, fused_device(): pl.pallas_call(layer_kernel, out_shape=(shape((2, TOK, D)), shape((2, TOK...  189 us
    pallas_call x1, Pallas kernels, fused_device(): pl.pallas_call(widen_kernel, out_shape=(shape((tok, 2, D)), shape((tok, 2...  5.65 us

profile of v6, /device:TPU:1, one launch (start us, length us, event | category | flops | bytes accessed | tf_op | source)
XLA Modules:
  0.0 195.9 jit_solution(12969992385645537334)
XLA Ops:
  0.7 189.1 %shard_map.271 = (bf16[2,160,1024]{2,1,0:T(8,128)(2,1)}, bf16[2,160,1024]{2,1,0:T(8,128)(2,1)}, bf16[4,128,768]{2,1,0:T(8,128)(2,1)}, bf16[128,1024]{1,0:T(8,128...) custom-call(bf16[146,2,1024]{2,1,0:T(2,128)(2,1)} %bitcast.13, ...), custom_call_target="tpu_custom_call" | custom-call | flops 25999998976 | bytes 30000000 | tf_op jit(solution)/shard_map/pallas_call | solution.py:1165
  189.8 5.6 %shard_map.272 = (bf16[146,2,1024]{2,1,0:T(2,128)(2,1)}, bf16[146,2,1024]{2,1,0:T(2,128)(2,1)}, f32[128]{0:T(128)}, f32[128]{0:T(128)}, f32[128,3072]{1,0:T(8,12...) custom-call(bf16[2,160,1024]{2,1,0:T(8,128)(2,1)} %get-tuple-element, ...), custom_call_target="tpu_custom_call" | custom-call | tf_op jit(solution)/shard_map/pallas_call | solution.py:1227
